TPU v7x, 32 devices: a whole 2x2x4 slice. The times are simulated.
32 devices in a mesh: blk: 8 (over z, y), rep: 4 (over x, core).
Axes of the slice: x: 2, y: 2, z: 4, core: 2. Of those that a mesh axis runs over, the one named last changes fastest.
Arguments:
- image_feats: bfloat16 [16384, 1152], P(('blk', 'rep')), may hold values from -16 to 16, as said below
- text_feats: bfloat16 [16384, 1152], P(('blk', 'rep')), may hold values from -16 to 16, as said below
- head: bfloat16 [1152, 1152], replicated, may hold values from -0.1875 to 0.1875
- image_ids: int32 [16384], P(('blk', 'rep')), may hold values from 0 to 2047
- text_ids: int32 [16384], P(('blk', 'rep')), may hold values from 0 to 2047
- log_scale: float32 [1], replicated, may hold values from 3 to 3.7
- bias: float32 [1], replicated, may hold values from -3 to -1
Outputs:
- grad_image_feats: bfloat16 [16384, 1152], P(('blk', 'rep'))
- grad_text_feats: bfloat16 [16384, 1152], P(('blk', 'rep'))
- grad_head: float32 [1152, 1152], P('blk')
Inputs may be any that keep to these rules, and one draw needn't show every extreme that they name: `image_feats`: row magnitudes differ from row to row. `text_feats`: row magnitudes differ from row to row.
All inputs are finite; a program needn't handle non-finite values.
Results may differ from a plain program's by a relative error of at most 0.0072.
Values may be sent and summed in bfloat16 or wider, within the bound.
A program may use at most 128 MiB of HBM per device.

v0:
```python
import jax
import jax.numpy as jnp
from jax import lax
from jax.sharding import PartitionSpec as P

HOPS = 4


def shifted(value, axis, steps):
    count = lax.axis_size(axis)
    pairs = [(source, (source + steps) % count) for source in range(count)]
    return lax.ppermute(value, axis, pairs)


def unit_rows(values):
    inverse = lax.rsqrt(jnp.sum(values * values, axis=-1, keepdims=True) + 1e-06)
    return (values * inverse, inverse)


def per_device(image_feats, text_feats, head, image_ids, text_ids, log_scale, bias):
    u_local = jnp.dot(image_feats, head, preferred_element_type=jnp.float32)
    x_full, inv_u = unit_rows(u_local)
    x_half = x_full.astype(jnp.bfloat16)
    y_full, inv_t = unit_rows(text_feats.astype(jnp.float32))
    y_half = y_full.astype(jnp.bfloat16)
    scale = jnp.exp(log_scale[0])
    offset = bias[0]

    def coefficients(images, image_labels, texts, text_labels):
        logits = (
            scale * jnp.einsum("id,jd->ij", images, texts, preferred_element_type=jnp.float32)
            + offset
        )
        positive = (image_labels[:, None] == text_labels[None, :]).astype(jnp.float32)
        return (scale * (jax.nn.sigmoid(logits) - positive)).astype(jnp.bfloat16)

    def tile(block, block_ids):
        coef = coefficients(x_half, image_ids, block, block_ids)
        image_part = jnp.dot(coef, block, preferred_element_type=jnp.float32)
        text_part = jnp.einsum("ij,id->jd", coef, x_half, preferred_element_type=jnp.float32)
        return (image_part, text_part)

    grad_x, text_sum = tile(y_half, text_ids)
    block, block_ids = (y_half, text_ids)
    for hop in range(1, HOPS + 1):
        block = shifted(block, "blk", 1)
        block_ids = shifted(block_ids, "blk", 1)
        image_part, text_part = tile(block, block_ids)
        grad_x = grad_x + image_part
        text_sum = shifted(text_sum, "blk", 1) + text_part
    grad_y = shifted(text_sum, "blk", -HOPS)
    grad_u = (inv_u * (grad_x - x_full * jnp.sum(x_full * grad_x, axis=1, keepdims=True))).astype(
        jnp.bfloat16
    )
    grad_image = jnp.einsum("id,ed->ie", grad_u, head, preferred_element_type=jnp.float32).astype(
        jnp.bfloat16
    )
    cycle_rows = lax.psum_scatter(
        jnp.einsum("ie,id->ed", image_feats, grad_u, preferred_element_type=jnp.float32),
        "blk",
        scatter_dimension=0,
        tiled=True,
    )
    devices_all = lax.axis_size("blk") * lax.axis_size("rep")
    grad_head = lax.psum(cycle_rows, "rep") / devices_all
    grad_text = (
        inv_t * (grad_y - y_full * jnp.sum(y_full * grad_y, axis=1, keepdims=True))
    ).astype(jnp.bfloat16)
    return (grad_image, grad_text, grad_head)


def solution(mesh):
    placed = (
        P(("blk", "rep"), None),
        P(("blk", "rep"), None),
        P(),
        P(("blk", "rep")),
        P(("blk", "rep")),
        P(),
        P(),
    )
    return jax.shard_map(
        per_device,
        mesh=mesh,
        in_specs=placed,
        out_specs=(P(("blk", "rep"), None), P(("blk", "rep"), None), P("blk", None)),
        check_vma=False,
    )
```

profile of v0, /device:TPU:0, one launch (start us, length us, event | category | flops | bytes accessed | tf_op | source)
XLA Modules:
  0.0 568.3 jit_solution(8581260081599629317)
XLA Ops:
  7.2 1.7 fusion.7
  9.3 3.0 collective-permute-start
  12.3 1.5 collective-permute-start.1
  15.2 2.0 multiply_reduce_fusion.1
  17.1 24.2 %collective-permute-done = bf16[512,1152]{1,0:T(8,128)(2,1)S(1)} collective-permute-done((bf16[512,1152]{1,0:T(8,128)(2,1)S(1)}, bf16[512,1152]{1,0:T(8,128)(2,1)S(1)}, u32[]{:S(2)}, u32[]{:S(2)}) %collective-permute-start) | collective-permute-done | bytes 1179680 | tf_op jit(solution)/shard_map/ppermute | solution.py:12
  42.0 1.1 fusion.43
  43.1 1.2 collective-permute-start.3
  44.3 26.9 %collective-permute-done.2 = bf16[512,1152]{1,0:T(8,128)(2,1)S(1)} collective-permute-done((bf16[512,1152]{1,0:T(8,128)(2,1)S(1)}, bf16[512,1152]{1,0:T(8,128)(2,1)S(1)}, u32[]{:S(2)}, u32[]{:S(2)}) %collective-permute-start.2) | collective-permute-done | bytes 1179680 | tf_op jit(solution)/shard_map/ppermute | solution.py:12
  71.2 2.4 fusion.49
  74.4 76.3 %collective-permute-done.5 = s32[512]{0:T(512)S(1)} collective-permute-done((s32[512]{0:T(512)S(1)}, s32[512]{0:T(512)S(1)}, u32[]{:S(2)}, u32[]{:S(2)}) %collective-permute-start.5) | collective-permute-done | bytes 2080 | tf_op jit(solution)/shard_map/ppermute | solution.py:12
  150.8 1.1 fusion.44
  153.0 1.1 fusion.45
  155.0 1.1 fusion.46
  156.1 0.9 convolution_add_fusion.2
  157.1 23.9 %collective-permute-done.6 = bf16[512,1152]{1,0:T(8,128)(2,1)S(1)} collective-permute-done((bf16[512,1152]{1,0:T(8,128)(2,1)S(1)}, bf16[512,1152]{1,0:T(8,128)(2,1)S(1)}, u32[]{:S(2)}, u32[]{:S(2)}) %collective-permute-start.6) | collective-permute-done | bytes 1179680 | tf_op jit(solution)/shard_map/ppermute | solution.py:12
  181.0 1.1 fusion.47
  182.1 1.1 multiply_reduce_fusion
  183.7 1.0 copy-done.6
  184.7 4.1 convolution_bitcast_fusion
  188.8 6.9 %copy.12 = f32[1152,1152]{1,0:T(8,128)} copy(f32[1152,1152]{0,1:T(8,128)} %convolution_bitcast_fusion) | data formatting | bytes 10616832
  195.8 3.2 convolution_add_fusion
  199.9 95.1 %collective-permute-done.9 = f32[512,1152]{1,0:T(8,128)S(1)} collective-permute-done((f32[512,1152]{1,0:T(8,128)S(1)}, f32[512,1152]{1,0:T(8,128)S(1)}, u32[]{:S(2)}, u32[]{:S(2)}) %collective-permute-start.9) | collective-permute-done | bytes 2359328 | tf_op jit(solution)/shard_map/ppermute | solution.py:12
  296.3 50.0 %collective-permute-done.10 = f32[512,1152]{1,0:T(8,128)S(1)} collective-permute-done((f32[512,1152]{1,0:T(8,128)S(1)}, f32[512,1152]{1,0:T(8,128)S(1)}, u32[]{:S(2)}, u32[]{:S(2)}) %collective-permute-start.10) | collective-permute-done | bytes 2359328 | tf_op jit(solution)/shard_map/ppermute | solution.py:12
  347.7 55.1 %collective-permute-done.11 = f32[512,1152]{1,0:T(8,128)S(1)} collective-permute-done((f32[512,1152]{1,0:T(8,128)S(1)}, f32[512,1152]{1,0:T(8,128)S(1)}, u32[]{:S(2)}, u32[]{:S(2)}) %collective-permute-start.11) | collective-permute-done | bytes 2359328 | tf_op jit(solution)/shard_map/ppermute | solution.py:12
  403.2 2.9 convolution_convert_fusion
  406.1 104.4 %collective-permute-done.12 = f32[512,1152]{1,0:T(8,128)S(1)} collective-permute-done((f32[512,1152]{1,0:T(8,128)S(1)}, f32[512,1152]{1,0:T(8,128)S(1)}, u32[]{:S(2)}, u32[]{:S(2)}) %collective-permute-start.12) | collective-permute-done | bytes 2359328 | tf_op jit(solution)/shard_map/ppermute | solution.py:12
  510.5 1.4 copy-done.5
  512.4 2.5 copy.13
  514.8 3.5 fusion.6
  518.3 38.3 %all-reduce.2.cloned.1.call-done = f32[144,1152]{0,1:T(8,128)} async-done(((f32[144,1152]{0,1:T(8,128)}), f32[144,1152]{0,1:T(8,128)}) %all-reduce.2.cloned.1.call-update) | async-done | bytes 663568 | tf_op jit(solution)/shard_map/psum | solution.py:65
  556.6 2.3 broadcast_multiply_fusion
  559.0 2.4 copy.11
  (65 shorter events, 8.8 us)
Async XLA Ops:
  7.2 8.0 %copy-start = (bf16[1152,1152]{1,0:T(8,128)(2,1)S(1)}, bf16[1152,1152]{1,0:T(8,128)(2,1)}, u32[]{:S(2)}) copy-start(bf16[1152,1152]{1,0:T(8,128)(2,1)} %param.9) | copy-start | bytes 7962628
  7.2 505.2 %reduce-scatter.4.cloned.1.call-start = ((), (), s32[]{:S(2)}) async-start(), calls=%async_computation.2 | async-start | bytes 5971968
  7.2 1.8 copy-start.3
  9.0 3.3 copy-start.14
  9.0 6.2 %copy-start.13 = (bf16[512,1152]{1,0:T(8,128)(2,1)S(1)}, bf16[512,1152]{1,0:T(8,128)(2,1)}, u32[]{:S(2)}) copy-start(bf16[512,1152]{1,0:T(8,128)(2,1)} %param.7) | copy-start | bytes 3538948
  9.3 32.0 %collective-permute-start = (bf16[512,1152]{1,0:T(8,128)(2,1)S(1)}, bf16[512,1152]{1,0:T(8,128)(2,1)S(1)}, u32[]{:S(2)}, u32[]{:S(2)}) collective-permute-start(bf16[512,1152]{1,0:T(8,128)(2,1)S(1)} %fusion.2), channel_id=1, source_target_pairs={{0,4},{4,8},{8,12},{12,16},{16,20},{20,24},{24,28},{28,0},{1,5},{5... | collective-permute-start | bytes 3538952 | tf_op jit(solution)/shard_map/ppermute | solution.py:12
  12.3 30.8 %collective-permute-start.1 = (s32[512]{0:T(512)S(1)}, s32[512]{0:T(512)S(1)}, u32[]{:S(2)}, u32[]{:S(2)}) collective-permute-start(s32[512]{0:T(512)S(1)} %copy-done.14), channel_id=1, source_target_pairs={{0,4},{4,8},{8,12},{12,16},{16,20},{20,24},{24,28},{28,0},{1,5},{5... | collective-permute-start | bytes 6152 | tf_op jit(solution)/shard_map/ppermute | solution.py:12
  41.3 29.9 %collective-permute-start.2 = (bf16[512,1152]{1,0:T(8,128)(2,1)S(1)}, bf16[512,1152]{1,0:T(8,128)(2,1)S(1)}, u32[]{:S(2)}, u32[]{:S(2)}) collective-permute-start(bf16[512,1152]{1,0:T(8,128)(2,1)S(1)} %collective-permute-done), channel_id=1, source_target_pairs={{0,4},{4,8},{8,12},{12,16},{16,20},{20,24},{24,28},{28,0},{1,5},{5... | collective-permute-start | bytes 3538952 | tf_op jit(solution)/shard_map/ppermute | solution.py:12
  41.3 0.7 copy-start.15
  41.5 139.5 %copy-start.1 = (bf16[512,1152]{1,0:T(8,128)(2,1)}, bf16[512,1152]{1,0:T(8,128)(2,1)S(1)}, u32[]{:S(2)}) copy-start(bf16[512,1152]{1,0:T(8,128)(2,1)S(1)} %multiply_convert_fusion.1) | copy-start | bytes 3538948
  43.1 30.4 %collective-permute-start.3 = (s32[512]{0:T(512)S(1)}, s32[512]{0:T(512)S(1)}, u32[]{:S(2)}, u32[]{:S(2)}) collective-permute-start(s32[512]{0:T(512)S(1)} %collective-permute-done.1), channel_id=1, source_target_pairs={{0,4},{4,8},{8,12},{12,16},{16,20},{20,24},{24,28},{28,0},{1,5},{5... | collective-permute-start | bytes 6152 | tf_op jit(solution)/shard_map/ppermute | solution.py:12
  71.2 81.6 %collective-permute-start.4 = (bf16[512,1152]{1,0:T(8,128)(2,1)S(1)}, bf16[512,1152]{1,0:T(8,128)(2,1)S(1)}, u32[]{:S(2)}, u32[]{:S(2)}) collective-permute-start(bf16[512,1152]{1,0:T(8,128)(2,1)S(1)} %collective-permute-done.2), channel_id=1, source_target_pairs={{0,4},{4,8},{8,12},{12,16},{16,20},{20,24},{24,28},{28,0},{1,5},{5... | collective-permute-start | bytes 3538952 | tf_op jit(solution)/shard_map/ppermute | solution.py:12
  73.5 122.2 %collective-permute-start.8 = (f32[512,1152]{1,0:T(8,128)}, f32[512,1152]{1,0:T(8,128)}, u32[]{:S(2)}, u32[]{:S(2)}) collective-permute-start(f32[512,1152]{1,0:T(8,128)} %fusion.49), channel_id=1, source_target_pairs={{0,4},{4,8},{8,12},{12,16},{16,20},{20,24},{24,28},{28,0},{1,5},{5... | collective-permute-start | bytes 7077896 | tf_op jit(solution)/shard_map/ppermute | solution.py:12
  73.5 77.2 %collective-permute-start.5 = (s32[512]{0:T(512)S(1)}, s32[512]{0:T(512)S(1)}, u32[]{:S(2)}, u32[]{:S(2)}) collective-permute-start(s32[512]{0:T(512)S(1)} %collective-permute-done.3), channel_id=1, source_target_pairs={{0,4},{4,8},{8,12},{12,16},{16,20},{20,24},{24,28},{28,0},{1,5},{5... | collective-permute-start | bytes 6152 | tf_op jit(solution)/shard_map/ppermute | solution.py:12
  150.8 6.3 %collective-permute-start.7 = (s32[512]{0:T(512)S(1)}, s32[512]{0:T(512)S(1)}, u32[]{:S(2)}, u32[]{:S(2)}) collective-permute-start(s32[512]{0:T(512)S(1)} %collective-permute-done.5), channel_id=1, source_target_pairs={{0,4},{4,8},{8,12},{12,16},{16,20},{20,24},{24,28},{28,0},{1,5},{5... | collective-permute-start | bytes 6152 | tf_op jit(solution)/shard_map/ppermute | solution.py:12
  151.9 0.9 copy-start.12
  152.8 28.2 %collective-permute-start.6 = (bf16[512,1152]{1,0:T(8,128)(2,1)S(1)}, bf16[512,1152]{1,0:T(8,128)(2,1)S(1)}, u32[]{:S(2)}, u32[]{:S(2)}) collective-permute-start(bf16[512,1152]{1,0:T(8,128)(2,1)S(1)} %collective-permute-done.4), channel_id=1, source_target_pairs={{0,4},{4,8},{8,12},{12,16},{16,20},{20,24},{24,28},{28,0},{1,5},{5... | collective-permute-start | bytes 3538952 | tf_op jit(solution)/shard_map/ppermute | solution.py:12
  154.1 0.9 copy-start.8
  182.1 1.1 copy-start.10
  183.7 1.0 copy-start.6
  195.7 361.0 %all-reduce.2.cloned.1.call-start = ((), (), s32[]{:S(2)}) async-start(), calls=%async_computation.1 | async-start | bytes 2359296 | tf_op jit(solution)/shard_map/psum | solution.py:65
  195.7 3.3 copy-start.2
  195.7 3.3 copy-start.9
  199.0 96.1 %collective-permute-start.9 = (f32[512,1152]{1,0:T(8,128)S(1)}, f32[512,1152]{1,0:T(8,128)S(1)}, u32[]{:S(2)}, u32[]{:S(2)}) collective-permute-start(f32[512,1152]{1,0:T(8,128)S(1)} %convolution_add_fusion), channel_id=1, source_target_pairs={{0,4},{4,8},{8,12},{12,16},{16,20},{20,24},{24,28},{28,0},{1,5},{5... | collective-permute-start | bytes 7077896 | tf_op jit(solution)/shard_map/ppermute | solution.py:12
  295.3 51.0 %collective-permute-start.10 = (f32[512,1152]{1,0:T(8,128)S(1)}, f32[512,1152]{1,0:T(8,128)S(1)}, u32[]{:S(2)}, u32[]{:S(2)}) collective-permute-start(f32[512,1152]{1,0:T(8,128)S(1)} %add.99), channel_id=1, source_target_pairs={{0,4},{4,8},{8,12},{12,16},{16,20},{20,24},{24,28},{28,0},{1,5},{5... | collective-permute-start | bytes 7077896 | tf_op jit(solution)/shard_map/ppermute | solution.py:12
  296.3 50.6 %copy-start.11 = (bf16[512,512]{1,0:T(8,128)(2,1)S(1)}, bf16[512,512]{1,0:T(8,128)(2,1)}, u32[]{:S(2)}) copy-start(bf16[512,512]{1,0:T(8,128)(2,1)} %copy-done.10) | copy-start | bytes 1572868
  346.6 56.3 %collective-permute-start.11 = (f32[512,1152]{1,0:T(8,128)S(1)}, f32[512,1152]{1,0:T(8,128)S(1)}, u32[]{:S(2)}, u32[]{:S(2)}) collective-permute-start(f32[512,1152]{1,0:T(8,128)S(1)} %add.100), channel_id=1, source_target_pairs={{0,4},{4,8},{8,12},{12,16},{16,20},{20,24},{24,28},{28,0},{1,5},{5... | collective-permute-start | bytes 7077896 | tf_op jit(solution)/shard_map/ppermute | solution.py:12
  347.7 55.4 %copy-start.7 = (bf16[512,1152]{1,0:T(8,128)(2,1)S(1)}, bf16[512,1152]{1,0:T(8,128)(2,1)}, u32[]{:S(2)}) copy-start(bf16[512,1152]{1,0:T(8,128)(2,1)} %copy-done.6) | copy-start | bytes 3538948
  403.1 108.8 %copy-start.4 = (bf16[512,1152]{1,0:T(8,128)(2,1)S(1)}, bf16[512,1152]{1,0:T(8,128)(2,1)}, u32[]{:S(2)}) copy-start(bf16[512,1152]{1,0:T(8,128)(2,1)} %param.8) | copy-start | bytes 3538948
  403.1 107.4 %collective-permute-start.12 = (f32[512,1152]{1,0:T(8,128)S(1)}, f32[512,1152]{1,0:T(8,128)S(1)}, u32[]{:S(2)}, u32[]{:S(2)}) collective-permute-start(f32[512,1152]{1,0:T(8,128)S(1)} %add.101), channel_id=1, source_target_pairs={{0,16},{4,20},{8,24},{12,28},{16,0},{20,4},{24,8},{28,12},{1,17},{... | collective-permute-start | bytes 7077896 | tf_op jit(solution)/shard_map/ppermute | solution.py:12
  510.5 1.4 copy-start.5
Sparse Core Ops, SparseCore 0:
  195.8 275.8 reduce-scatter.3
  515.0 41.6 all-reduce.1
where the time goes:
time: 569 us; the launch traced here: 568 us
  waiting for transfers between devices  494 us (87%)
  matrix products  27.2 us (5%)
  between operations  15.8 us (3%)
  local copies, waits for them, and re-layouts  14.7 us (3%)
  other arithmetic  9.63 us (2%)
  starting transfers between devices  6.5 us (1%)
    ppermute x13, waiting for transfers between devices, shifted(): return lax.ppermute(value, axis, pairs)  456 us
    psum x1, waiting for transfers between devices, per_device(): grad_head = lax.psum(cycle_rows, 'rep') / devices_all  38.3 us
    unnamed x35, local copies, waits for them, and re-layouts  14.7 us
  transfers between devices with their start and end apart: 15, of which 10 were waited for; matrix products, arithmetic and copies ran while one was open for 7% of the time, Pallas kernels for 0%

commit v1 on v0

v1 whole, which is shorter than its diff:
```python
import jax
import jax.numpy as jnp
from jax import lax
from jax.sharding import PartitionSpec as P

HOPS = 4


def shifted(value, axis, steps):
    count = lax.axis_size(axis)
    pairs = [(source, (source + steps) % count) for source in range(count)]
    return lax.ppermute(value, axis, pairs)


def swapped(value, axis, bit, senders=(0, 1)):
    count = lax.axis_size(axis)
    pairs = [(k, k ^ bit) for k in range(count) if (k // bit) % 2 in senders]
    return lax.ppermute(value, axis, pairs)


def after(value, *others):
    return lax.optimization_barrier((value, *others))[0]


def unit_rows(values):
    inverse = lax.rsqrt(jnp.sum(values * values, axis=-1, keepdims=True) + 1e-06)
    return (values * inverse, inverse)


def halved(value, axis, bit, dim):
    half = value.shape[dim] // 2
    mine = (lax.axis_index(axis) // bit) % 2
    send = lax.dynamic_slice_in_dim(value, (1 - mine) * half, half, dim).astype(jnp.bfloat16)
    keep = lax.dynamic_slice_in_dim(value, mine * half, half, dim)
    return keep + swapped(send, axis, bit).astype(jnp.float32)


def head_rows(partial):
    n_blk, n_rep = lax.axis_size("blk"), lax.axis_size("rep")
    rows, columns = partial.shape
    value = partial.reshape(n_blk, rows // n_blk, columns)
    split = []
    bit = 1
    while bit < n_rep:
        if value.shape[1] % 2 == 0:
            value = halved(value, "rep", bit, 1)
            split.append(bit)
        else:
            value = value + swapped(value, "rep", bit)
        bit *= 2
    bit = n_blk // 2
    while bit >= 1:
        value = halved(value, "blk", bit, 0)
        bit //= 2
    value = value[0] / (n_blk * n_rep)
    for bit in reversed(split):
        mine = (lax.axis_index("rep") // bit) % 2
        other = swapped(value, "rep", bit)
        first = jnp.where(mine == 0, value, other)
        second = jnp.where(mine == 0, other, value)
        value = jnp.concatenate([first, second], axis=0)
    return value


def per_device(image_feats, text_feats, head, image_ids, text_ids, log_scale, bias):
    n_blk = lax.axis_size("blk")
    me = lax.axis_index("blk")
    odd = me % 2 == 1
    scale = jnp.exp(log_scale[0])
    offset = bias[0]

    y_full, inv_t = unit_rows(text_feats.astype(jnp.float32))
    y_half = y_full.astype(jnp.bfloat16)
    ids = lax.all_gather(jnp.stack([image_ids, text_ids]), "blk")

    y_back2 = shifted(y_half, "blk", 2)
    u_local = jnp.dot(image_feats, head, preferred_element_type=jnp.float32)
    x_full, inv_u = unit_rows(u_local)
    x_half = x_full.astype(jnp.bfloat16)
    own_pair = swapped(jnp.where(odd, x_half, y_half), "blk", 1)
    y_back4 = shifted(y_back2, "blk", 2)
    y_cross2 = swapped(y_back2, "blk", 1)
    y_cross4 = swapped(y_back4, "blk", 1, (1,))

    x_fore2 = shifted(after(x_half, y_back4), "blk", -2)
    x_fore4 = shifted(x_fore2, "blk", -2)
    x_cross2 = swapped(x_fore2, "blk", 1)
    x_cross4 = swapped(x_fore4, "blk", 1, (0,))

    def labels(kind, step):
        return lax.dynamic_index_in_dim(ids, (me + step + n_blk) % n_blk, 0, False)[kind]

    def coefficients(images, image_labels, texts, text_labels):
        logits = (
            scale * jnp.einsum("id,jd->ij", images, texts, preferred_element_type=jnp.float32)
            + offset
        )
        positive = (image_labels[:, None] == text_labels[None, :]).astype(jnp.float32)
        return (scale * (jax.nn.sigmoid(logits) - positive)).astype(jnp.bfloat16)

    def image_part(texts, step):
        coef = coefficients(x_half, image_ids, texts, labels(1, step))
        return jnp.dot(coef, texts, preferred_element_type=jnp.float32)

    def text_part(images, step):
        coef = coefficients(images, labels(0, step), y_half, text_ids)
        return jnp.einsum("ij,id->jd", coef, images, preferred_element_type=jnp.float32)

    own = coefficients(x_half, image_ids, y_half, text_ids)
    grad_x = jnp.dot(own, y_half, preferred_element_type=jnp.float32)
    grad_y = jnp.einsum("ij,id->jd", own, x_half, preferred_element_type=jnp.float32)

    grad_x = grad_x + image_part(y_back2, -2)
    grad_x = grad_x + image_part(y_cross2, jnp.where(odd, -3, -1))
    grad_x = grad_x + image_part(y_back4, -4)
    grad_x = grad_x + image_part(jnp.where(odd, own_pair, y_cross4), jnp.where(odd, -1, -3))

    grad_u = (inv_u * (grad_x - x_full * jnp.sum(x_full * grad_x, axis=1, keepdims=True))).astype(
        jnp.bfloat16
    )
    grad_head = head_rows(
        jnp.einsum("ie,id->ed", image_feats, grad_u, preferred_element_type=jnp.float32)
    )
    grad_image = jnp.einsum("id,ed->ie", grad_u, head, preferred_element_type=jnp.float32).astype(
        jnp.bfloat16
    )

    grad_y = grad_y + text_part(x_fore2, 2)
    grad_y = grad_y + text_part(x_cross2, jnp.where(odd, 1, 3))
    grad_y = grad_y + text_part(x_fore4, 4)
    grad_y = grad_y + text_part(jnp.where(odd, x_cross4, own_pair), jnp.where(odd, 3, 1))
    grad_text = (
        inv_t * (grad_y - y_full * jnp.sum(y_full * grad_y, axis=1, keepdims=True))
    ).astype(jnp.bfloat16)
    return (grad_image, grad_text, grad_head)


def solution(mesh):
    placed = (
        P(("blk", "rep"), None),
        P(("blk", "rep"), None),
        P(),
        P(("blk", "rep")),
        P(("blk", "rep")),
        P(),
        P(),
    )
    return jax.shard_map(
        per_device,
        mesh=mesh,
        in_specs=placed,
        out_specs=(P(("blk", "rep"), None), P(("blk", "rep"), None), P("blk", None)),
        check_vma=False,
    )
```

time: 569 us -> 258 us (0.45)
  waiting for transfers between devices: 494 us -> 73.7 us
  blocking collectives: 0 us -> 68 us
  matrix products: 27.2 us -> 65 us
  starting transfers between devices: 6.5 us -> 20.3 us
  between operations: 15.8 us -> 2.3 us
  other arithmetic: 9.63 us -> 16.1 us
    ppermute x13 -> x4, waiting for transfers between devices: 456 us -> 61.6 us  [shifted(): return lax.ppermute(value, axis, pairs)]
    all_gather x0 -> x1, blocking collectives: none -> 68 us  [per_device(): ids = lax.all_gather(jnp.stack([image_ids, text_ids]), 'blk')]
    dot_general x10, matrix products: 12.8 us -> 54.1 us  [the longest x4 24.8 us: text_part(): jnp.einsum('ij,id->jd', coef, images, preferred_element_type=jnp.float32)]
    psum x1 -> x0, waiting for transfers between devices: 38.3 us -> none  [per_device(): grad_head = lax.psum(cycle_rows, 'rep') / devices_all]
    ppermute x0 -> x12, starting transfers between devices: none -> 12.6 us  [swapped(): return lax.ppermute(value, axis, pairs)]
    ppermute x0 -> x12, waiting for transfers between devices: none -> 12.1 us  [swapped(): return lax.ppermute(value, axis, pairs)]
    unnamed x35 -> x34, local copies, waits for them, and re-layouts: 14.7 us -> 8.32 us
  transfers between devices with their start and end apart: 15 -> 16, of which waited for: 10 -> 6; matrix products, arithmetic and copies ran while one was open for 7% -> 25% of each run, Pallas kernels for 0% -> 0%
where the time goes in v1:
time: 258 us; the launch traced here: 257 us
  waiting for transfers between devices  73.7 us (29%)
  blocking collectives  68 us (26%)
  matrix products  65 us (25%)
  starting transfers between devices  20.3 us (8%)
  other arithmetic  16.1 us (6%)
  local copies, waits for them, and re-layouts  11.8 us (5%)
    all_gather x1, blocking collectives, per_device(): ids = lax.all_gather(jnp.stack([image_ids, text_ids]), 'blk')  68 us
    ppermute x4, waiting for transfers between devices, shifted(): return lax.ppermute(value, axis, pairs)  61.6 us
    dot_general x4, matrix products, text_part(): jnp.einsum('ij,id->jd', coef, images, preferred_element_type=jnp.float32)  24.8 us
    dot_general x4, matrix products, image_part(): return jnp.dot(coef, texts, preferred_element_type=jnp.float32)  24.6 us
    ppermute x12, starting transfers between devices, swapped(): return lax.ppermute(value, axis, pairs)  12.6 us
    ppermute x12, waiting for transfers between devices, swapped(): return lax.ppermute(value, axis, pairs)  12.1 us
    unnamed x34, local copies, waits for them, and re-layouts  8.32 us
    ppermute x4, starting transfers between devices, shifted(): return lax.ppermute(value, axis, pairs)  7.62 us
  transfers between devices with their start and end apart: 16, of which 6 were waited for; matrix products, arithmetic and copies ran while one was open for 25% of the time, Pallas kernels for 0%

profile of v1, /device:TPU:0, one launch (start us, length us, event | category | flops | bytes accessed | tf_op | source)
XLA Modules:
  0.0 257.2 jit_solution(8941045566205962773)
XLA Ops:
  0.7 1.7 fusion.9
  2.7 3.3 %multiply_reduce_fusion.1 = (f32[512]{0:T(512)S(1)}, f32[512,1152]{1,0:T(8,128)S(1)}) fusion(bf16[512,1152]{1,0:T(8,128)(2,1)} %param.7, bf16[1152,1152]{1,0:T(8,128)(2,1)S(1)} %copy-done), kind=kOutput, calls=%fused_computation.23 | convolution fusion | flops 1360133632 | bytes 6195200 | tf_op jit(solution)/shard_map/dot_general | solution.py:77
  6.1 2.1 broadcast_select_fusion.2
  9.3 3.0 %collective-permute-start = (bf16[512,1152]{1,0:T(8,128)(2,1)S(1)}, bf16[512,1152]{1,0:T(8,128)(2,1)}, u32[]{:S(2)}, u32[]{:S(2)}) collective-permute-start(bf16[512,1152]{1,0:T(8,128)(2,1)S(1)} %get-tuple-element.7), channel_id=1, source_target_pairs={{0,8},{4,12},{8,16},{12,20},{16,24},{20,28},{24,0},{28,4},{1,9},{5... | collective-permute-start | bytes 3538952 | tf_op jit(solution)/shard_map/ppermute | solution.py:12
  12.3 28.1 %collective-permute-done = bf16[512,1152]{1,0:T(8,128)(2,1)} collective-permute-done((bf16[512,1152]{1,0:T(8,128)(2,1)S(1)}, bf16[512,1152]{1,0:T(8,128)(2,1)}, u32[]{:S(2)}, u32[]{:S(2)}) %collective-permute-start) | collective-permute-done | bytes 1179680 | tf_op jit(solution)/shard_map/ppermute | solution.py:12
  43.3 2.8 %fusion.73 = bf16[512,512]{1,0:T(8,128)(2,1)S(1)} fusion(bf16[512,1152]{1,0:T(8,128)(2,1)} %get-tuple-element.4, bf16[512,1152]{1,0:T(8,128)(2,1)} %copy-done.8, s32[512]{0:T(512)S(1)} %copy-done.15, f32[]{:T(128)} %bitcast.56, f32[]{:T(128)} %bitcast, s32[512]{0:T(512)S(1)} %copy-done.14), kind=kOutput, calls=%fused_computation.99 | convolution fusion | flops 606601216 | bytes 2887688 | tf_op jit(solution)/shard_map/id,jd->ij/dot_general | solution.py:95
  46.1 2.4 fusion.137
  49.0 68.0 %all-gather.1 = s32[8,2,512]{2,1,0:T(2,128)S(1)} all-gather(s32[1,2,512]{2,1,0:T(2,128)S(1)} %add_bitcast_fusion), channel_id=2, replica_groups=mesh['blk'=8,'rep'=4] {'blk'}, dimensions={0}, use_global_device_ids=true | all-gather | bytes 36864 | tf_op jit(solution)/shard_map/all_gather | solution.py:74
  118.6 6.0 %convolution_add_fusion.5 = f32[512,1152]{1,0:T(8,128)} fusion(f32[512,1152]{1,0:T(8,128)} %fusion.137, bf16[512,1152]{1,0:T(8,128)(2,1)} %collective-permute-done, bf16[512,1152]{1,0:T(8,128)(2,1)} %get-tuple-element.4, s32[512]{0:T(512)S(1)} %bitcast.75, f32[]{:T(128)} %bitcast.64, f32[]{:T(128)} %bitcast, s32[512]{0:T(512)S(1)} %copy-done.14), kind=kOutput, calls=%fused_computation.5 | convolution fusion | flops 1211170816 | bytes 7081992 | tf_op jit(solution)/shard_map/dot_general | solution.py:103
  124.6 5.2 %fusion.83 = f32[512,1152]{1,0:T(8,128)} fusion(bf16[512,1152]{1,0:T(8,128)(2,1)} %collective-permute-done.2, bf16[512,1152]{1,0:T(8,128)(2,1)} %get-tuple-element.4, s32[512]{0:T(512)S(1)} %bitcast.74, f32[]{:T(128)} %bitcast.62, f32[]{:T(128)} %bitcast, s32[512]{0:T(512)S(1)} %copy-done.14), kind=kOutput, calls=%fused_computation.112 | convolution fusion | flops 1210580992 | bytes 4722696 | tf_op jit(solution)/shard_map/dot_general | solution.py:103
  129.7 6.7 %fusion = f32[512,1152]{1,0:T(8,128)} fusion(f32[512,1152]{1,0:T(8,128)} %fusion.83, f32[512,1152]{1,0:T(8,128)} %convolution_add_fusion.5, bf16[512,1152]{1,0:T(8,128)(2,1)} %collective-permute-done.1, bf16[512,1152]{1,0:T(8,128)(2,1)} %get-tuple-element.4, s32[512]{0:T(512)S(1)} %bitcast.73, f32[]{:T(128)} %bitcast.63, f32[]{:T(128)} %bitcast, ...), kind=kOutput, calls=%fused_computation.6 | convolution fusion | flops 1211760640 | bytes 9441288 | tf_op jit(solution)/shard_map/dot_general | solution.py:103
  136.4 4.1 %collective-permute-done.4 = bf16[512,1152]{1,0:T(8,128)(2,1)} collective-permute-done((bf16[512,1152]{1,0:T(8,128)(2,1)}, bf16[512,1152]{1,0:T(8,128)(2,1)}, u32[]{:S(2)}, u32[]{:S(2)}) %collective-permute-start.4) | collective-permute-done | bytes 1179680 | tf_op jit(solution)/shard_map/ppermute | solution.py:18
  140.5 6.8 %multiply_reduce_fusion = (f32[512]{0:T(512)S(1)}, f32[512,1152]{1,0:T(8,128)}) fusion(f32[512,1152]{1,0:T(8,128)} %copy-done.4, f32[512]{0:T(512)S(1)} %get-tuple-element.27, f32[512,1152]{1,0:T(8,128)} %fusion, bf16[512,1152]{1,0:T(8,128)(2,1)} %collective-permute-done.3, bf16[512,1152]{1,0:T(8,128)(2,1)} %collective-permute-done.4, pred[]{:T(512)S(6)} %eq.151, ...), kind=kOutput, calls=%fused_computation.22 | convolution fusion | flops 1214119424 | bytes 10625033 | tf_op jit(solution)/shard_map/dot_general | solution.py:103
  147.3 2.9 %multiply_convert_fusion = bf16[512,1152]{1,0:T(8,128)(2,1)S(1)} fusion(f32[512,1152]{1,0:T(8,128)} %get-tuple-element.23, f32[512,1152]{1,0:T(8,128)} %copy-done.4, f32[512]{0:T(512)S(1)} %get-tuple-element.22, f32[512]{0:T(512)S(1)} %get-tuple-element.27), kind=kLoop, calls=%fused_computation.21 | loop fusion | flops 2949120 | bytes 5902336 | tf_op jit(solution)/shard_map/convert_element_type | solution.py:118
  150.2 1.8 fusion.139
  152.1 2.3 copy-done.1
  157.1 1.9 constant_dynamic-slice_fusion.1
  159.1 1.9 copy_add_fusion
  164.9 2.3 fusion.138
  167.2 17.2 %collective-permute-done.5 = bf16[512,1152]{1,0:T(8,128)(2,1)} collective-permute-done((bf16[512,1152]{1,0:T(8,128)(2,1)}, bf16[512,1152]{1,0:T(8,128)(2,1)}, u32[]{:S(2)}, u32[]{:S(2)}) %collective-permute-start.5) | collective-permute-done | bytes 1179680 | tf_op jit(solution)/shard_map/ppermute | solution.py:12
  184.4 3.2 %collective-permute-start.7 = (bf16[512,1152]{1,0:T(8,128)(2,1)}, bf16[512,1152]{1,0:T(8,128)(2,1)}, u32[]{:S(2)}, u32[]{:S(2)}) collective-permute-start(bf16[512,1152]{1,0:T(8,128)(2,1)} %collective-permute-done.5), channel_id=1, source_target_pairs={{0,24},{4,28},{8,0},{12,4},{16,8},{20,12},{24,16},{28,20},{1,25},{... | collective-permute-start | bytes 3538952 | tf_op jit(solution)/shard_map/ppermute | solution.py:12
  187.6 6.1 %convolution_add_fusion.2 = f32[512,1152]{1,0:T(8,128)} fusion(f32[512,1152]{1,0:T(8,128)} %fusion.138, bf16[512,1152]{1,0:T(8,128)(2,1)} %collective-permute-done.5, bf16[512,1152]{1,0:T(8,128)(2,1)} %copy-done.8, s32[512]{0:T(512)S(1)} %copy-done.15, f32[]{:T(128)} %bitcast.60, f32[]{:T(128)} %bitcast, s32[512]{0:T(512)S(1)} %bitcast.71), kind=kOutput, calls=%fused_computation.2 | convolution fusion | flops 1211170816 | bytes 7081992 | tf_op jit(solution)/shard_map/ij,id->jd/dot_general | solution.py:107
  193.7 1.7 convert_add_fusion
  195.6 2.9 %convolution_convert_fusion = bf16[512,1152]{1,0:T(8,128)(2,1)} fusion(bf16[512,1152]{1,0:T(8,128)(2,1)S(1)} %copy-done.7, bf16[1152,1152]{1,0:T(8,128)(2,1)S(1)} %copy-done), kind=kOutput, calls=%fused_computation.8 | convolution fusion | flops 1359544320 | bytes 5013504 | tf_op jit(solution)/shard_map/id,ed->ie/dot_general | solution.py:124
  198.6 16.3 %collective-permute-done.7 = bf16[512,1152]{1,0:T(8,128)(2,1)} collective-permute-done((bf16[512,1152]{1,0:T(8,128)(2,1)}, bf16[512,1152]{1,0:T(8,128)(2,1)}, u32[]{:S(2)}, u32[]{:S(2)}) %collective-permute-start.7) | collective-permute-done | bytes 1179680 | tf_op jit(solution)/shard_map/ppermute | solution.py:12
  214.9 2.6 %collective-permute-start.8 = (bf16[512,1152]{1,0:T(8,128)(2,1)}, bf16[512,1152]{1,0:T(8,128)(2,1)}, u32[]{:S(2)}, u32[]{:S(2)}) collective-permute-start(bf16[512,1152]{1,0:T(8,128)(2,1)} %collective-permute-done.7), channel_id=1, source_target_pairs={{0,4},{8,12},{16,20},{24,28},{1,5},{9,13},{17,21},{25,29},{2,6},{1... | collective-permute-start | bytes 3538952 | tf_op jit(solution)/shard_map/ppermute | solution.py:18
  217.5 7.9 %collective-permute-done.11 = bf16[4,36,1152]{2,0,1:T(4,128)(2,1)S(1)} collective-permute-done((bf16[4,36,1152]{2,0,1:T(4,128)(2,1)S(1)}, bf16[4,36,1152]{2,0,1:T(4,128)(2,1)S(1)}, u32[]{:S(2)}, u32[]{:S(2)}) %collective-permute-start.11) | collective-permute-done | bytes 331808 | tf_op jit(solution)/shard_map/ppermute | solution.py:18
  225.8 3.3 %collective-permute-start.12 = (bf16[2,36,1152]{2,0,1:T(2,128)(2,1)S(1)}, bf16[2,36,1152]{2,0,1:T(2,128)(2,1)}, u32[]{:S(2)}, u32[]{:S(2)}) collective-permute-start(bf16[2,36,1152]{2,0,1:T(2,128)(2,1)S(1)} %dynamic-slice_convert_fusion.2), channel_id=1, source_target_pairs={{0,8},{4,12},{8,0},{12,4},{16,24},{20,28},{24,16},{28,20},{1,9},{5... | collective-permute-start | bytes 497672 | tf_op jit(solution)/shard_map/ppermute | solution.py:18
  229.1 5.5 %fusion.82 = f32[512,1152]{1,0:T(8,128)} fusion(bf16[512,1152]{1,0:T(8,128)(2,1)} %collective-permute-done.7, bf16[512,1152]{1,0:T(8,128)(2,1)} %copy-done.8, s32[512]{0:T(512)S(1)} %copy-done.15, f32[]{:T(128)} %bitcast.58, f32[]{:T(128)} %bitcast, s32[512]{0:T(512)S(1)} %bitcast.70), kind=kOutput, calls=%fused_computation.111 | convolution fusion | flops 1210580992 | bytes 4722696 | tf_op jit(solution)/shard_map/ij,id->jd/dot_general | solution.py:107
  236.6 6.8 %fusion.1 = f32[512,1152]{1,0:T(8,128)} fusion(f32[512,1152]{1,0:T(8,128)} %fusion.82, f32[512,1152]{1,0:T(8,128)} %convolution_add_fusion.2, bf16[512,1152]{1,0:T(8,128)(2,1)} %collective-permute-done.6, bf16[512,1152]{1,0:T(8,128)(2,1)} %copy-done.8, s32[512]{0:T(512)S(1)} %copy-done.15, f32[]{:T(128)} %bitcast.59, f32[]{:T(128)} %bitcast, s32[512]{0:T(512)S(1)} %bitcast.69), kind=kOutput, calls=%fused_computation.7 | convolution fusion | flops 1211760640 | bytes 9441288 | tf_op jit(solution)/shard_map/ij,id->jd/dot_general | solution.py:107
  245.3 6.5 %fusion.5 = (f32[512]{0:T(512)S(1)}, f32[512,1152]{1,0:T(8,128)}) fusion(bf16[512,1152]{1,0:T(8,128)(2,1)} %param.8, f32[512]{0:T(512)S(1)} %get-tuple-element.26, f32[512,1152]{1,0:T(8,128)} %fusion.1, bf16[512,1152]{1,0:T(8,128)(2,1)} %collective-permute-done.8, bf16[512,1152]{1,0:T(8,128)(2,1)} %collective-permute-done.3, pred[]{:T(512)S(6)} %eq.151, ...), kind=kOutput, calls=%fused_computation.16 | convolution fusion | flops 1214709248 | bytes 9445385 | tf_op jit(solution)/shard_map/ij,id->jd/dot_general | solution.py:107
  253.1 3.2 %fusion.8 = bf16[512,1152]{1,0:T(8,128)(2,1)} fusion(f32[512,1152]{1,0:T(8,128)} %get-tuple-element.25, bf16[512,1152]{1,0:T(8,128)(2,1)S(1)} %copy-done.3, f32[512]{0:T(512)S(1)} %get-tuple-element.24, f32[512]{0:T(512)S(1)} %get-tuple-element.26), kind=kLoop, calls=%fused_computation.19 | loop fusion | flops 3538944 | bytes 4722688 | tf_op jit(solution)/shard_map/convert_element_type | solution.py:134
  (71 shorter events, 18.4 us)
Async XLA Ops:
  0.6 2.1 copy-start
  2.7 3.3 %copy-start.2 = (bf16[512,1152]{1,0:T(8,128)(2,1)S(1)}, bf16[512,1152]{1,0:T(8,128)(2,1)}, u32[]{:S(2)}) copy-start(bf16[512,1152]{1,0:T(8,128)(2,1)} %param.8) | copy-start | bytes 3538948
  6.0 2.2 copy-start.4
  6.1 37.2 %copy-start.14 = (s32[512]{0:T(512)S(1)}, s32[512]{0:T(512)}, u32[]{:S(2)}) copy-start(s32[512]{0:T(512)} %param.10) | copy-start | bytes 6148
  6.1 37.2 %copy-start.15 = (s32[512]{0:T(512)S(1)}, s32[512]{0:T(512)}, u32[]{:S(2)}) copy-start(s32[512]{0:T(512)} %param.11) | copy-start | bytes 6148
  8.2 1.0 copy-start.8
  9.3 31.1 %collective-permute-start = (bf16[512,1152]{1,0:T(8,128)(2,1)S(1)}, bf16[512,1152]{1,0:T(8,128)(2,1)}, u32[]{:S(2)}, u32[]{:S(2)}) collective-permute-start(bf16[512,1152]{1,0:T(8,128)(2,1)S(1)} %get-tuple-element.7), channel_id=1, source_target_pairs={{0,8},{4,12},{8,16},{12,20},{16,24},{20,28},{24,0},{28,4},{1,9},{5... | collective-permute-start | bytes 3538952 | tf_op jit(solution)/shard_map/ppermute | solution.py:12
  40.4 76.7 %collective-permute-start.2 = (bf16[512,1152]{1,0:T(8,128)(2,1)}, bf16[512,1152]{1,0:T(8,128)(2,1)}, u32[]{:S(2)}, u32[]{:S(2)}) collective-permute-start(bf16[512,1152]{1,0:T(8,128)(2,1)} %collective-permute-done), channel_id=1, source_target_pairs={{0,8},{4,12},{8,16},{12,20},{16,24},{20,28},{24,0},{28,4},{1,9},{5... | collective-permute-start | bytes 3538952 | tf_op jit(solution)/shard_map/ppermute | solution.py:12
  40.4 96.0 %collective-permute-start.3 = (bf16[512,1152]{1,0:T(8,128)(2,1)}, bf16[512,1152]{1,0:T(8,128)(2,1)}, u32[]{:S(2)}, u32[]{:S(2)}) collective-permute-start(bf16[512,1152]{1,0:T(8,128)(2,1)} %get-tuple-element.5), channel_id=1, source_target_pairs={{0,4},{4,0},{8,12},{12,8},{16,20},{20,16},{24,28},{28,24},{1,5},{5... | collective-permute-start | bytes 3538952 | tf_op jit(solution)/shard_map/ppermute | solution.py:18
  43.3 2.8 %copy-start.9 = (bf16[512,1152]{1,0:T(8,128)(2,1)S(1)}, bf16[512,1152]{1,0:T(8,128)(2,1)}, u32[]{:S(2)}) copy-start(bf16[512,1152]{1,0:T(8,128)(2,1)} %copy-done.8) | copy-start | bytes 3538948
  48.5 81.2 %collective-permute-start.1 = (bf16[512,1152]{1,0:T(8,128)(2,1)}, bf16[512,1152]{1,0:T(8,128)(2,1)}, u32[]{:S(2)}, u32[]{:S(2)}) collective-permute-start(bf16[512,1152]{1,0:T(8,128)(2,1)} %collective-permute-done), channel_id=1, source_target_pairs={{0,4},{4,0},{8,12},{12,8},{16,20},{20,16},{24,28},{28,24},{1,5},{5... | collective-permute-start | bytes 3538952 | tf_op jit(solution)/shard_map/ppermute | solution.py:18
  117.1 23.4 %collective-permute-start.4 = (bf16[512,1152]{1,0:T(8,128)(2,1)}, bf16[512,1152]{1,0:T(8,128)(2,1)}, u32[]{:S(2)}, u32[]{:S(2)}) collective-permute-start(bf16[512,1152]{1,0:T(8,128)(2,1)} %collective-permute-done.2), channel_id=1, source_target_pairs={{4,0},{12,8},{20,16},{28,24},{5,1},{13,9},{21,17},{29,25},{6,2},{1... | collective-permute-start | bytes 3538952 | tf_op jit(solution)/shard_map/ppermute | solution.py:18
  147.3 2.9 %copy-start.13 = (bf16[512,1152]{1,0:T(8,128)(2,1)S(1)}, bf16[512,1152]{1,0:T(8,128)(2,1)}, u32[]{:S(2)}) copy-start(bf16[512,1152]{1,0:T(8,128)(2,1)} %param.7) | copy-start | bytes 3538948
  150.2 1.8 copy-start.6
  152.1 2.3 copy-start.1
  155.7 3.4 %collective-permute-start.9 = (bf16[8,72,1152]{2,0,1:T(8,128)(2,1)}, bf16[8,72,1152]{2,0,1:T(8,128)(2,1)}, u32[]{:S(2)}, u32[]{:S(2)}) collective-permute-start(bf16[8,72,1152]{2,0,1:T(8,128)(2,1)} %copy.22), channel_id=1, source_target_pairs={{0,1},{1,0},{2,3},{3,2},{4,5},{5,4},{6,7},{7,6},{8,9},{9,8},{10,11... | collective-permute-start | bytes 3981320 | tf_op jit(solution)/shard_map/ppermute | solution.py:18
  155.7 28.7 %collective-permute-start.5 = (bf16[512,1152]{1,0:T(8,128)(2,1)}, bf16[512,1152]{1,0:T(8,128)(2,1)}, u32[]{:S(2)}, u32[]{:S(2)}) collective-permute-start(bf16[512,1152]{1,0:T(8,128)(2,1)} %get-tuple-element.4), channel_id=1, source_target_pairs={{0,24},{4,28},{8,0},{12,4},{16,8},{20,12},{24,16},{28,20},{1,25},{... | collective-permute-start | bytes 3538952 | tf_op jit(solution)/shard_map/ppermute | solution.py:12
  161.0 1.5 copy-start.5
  162.5 2.4 copy-start.10
  163.4 30.3 %collective-permute-start.10 = (bf16[8,36,1152]{2,0,1:T(8,128)(2,1)}, bf16[8,36,1152]{2,0,1:T(8,128)(2,1)}, u32[]{:S(2)}, u32[]{:S(2)}) collective-permute-start(bf16[8,36,1152]{2,0,1:T(8,128)(2,1)} %dynamic-slice_convert_fusion), channel_id=1, source_target_pairs={{0,2},{1,3},{2,0},{3,1},{4,6},{5,7},{6,4},{7,5},{8,10},{9,11},{10,... | collective-permute-start | bytes 1990664 | tf_op jit(solution)/shard_map/ppermute | solution.py:18
  184.4 30.5 %collective-permute-start.7 = (bf16[512,1152]{1,0:T(8,128)(2,1)}, bf16[512,1152]{1,0:T(8,128)(2,1)}, u32[]{:S(2)}, u32[]{:S(2)}) collective-permute-start(bf16[512,1152]{1,0:T(8,128)(2,1)} %collective-permute-done.5), channel_id=1, source_target_pairs={{0,24},{4,28},{8,0},{12,4},{16,8},{20,12},{24,16},{28,20},{1,25},{... | collective-permute-start | bytes 3538952 | tf_op jit(solution)/shard_map/ppermute | solution.py:12
  187.6 49.0 %collective-permute-start.6 = (bf16[512,1152]{1,0:T(8,128)(2,1)}, bf16[512,1152]{1,0:T(8,128)(2,1)}, u32[]{:S(2)}, u32[]{:S(2)}) collective-permute-start(bf16[512,1152]{1,0:T(8,128)(2,1)} %collective-permute-done.5), channel_id=1, source_target_pairs={{0,4},{4,0},{8,12},{12,8},{16,20},{20,16},{24,28},{28,24},{1,5},{5... | collective-permute-start | bytes 3538952 | tf_op jit(solution)/shard_map/ppermute | solution.py:18
  193.7 2.0 copy-start.7
  195.6 29.9 %collective-permute-start.11 = (bf16[4,36,1152]{2,0,1:T(4,128)(2,1)S(1)}, bf16[4,36,1152]{2,0,1:T(4,128)(2,1)S(1)}, u32[]{:S(2)}, u32[]{:S(2)}) collective-permute-start(bf16[4,36,1152]{2,0,1:T(4,128)(2,1)S(1)} %dynamic-slice_convert_fusion.1), channel_id=1, source_target_pairs={{0,16},{4,20},{8,24},{12,28},{16,0},{20,4},{24,8},{28,12},{1,17},{... | collective-permute-start | bytes 995336 | tf_op jit(solution)/shard_map/ppermute | solution.py:18
  214.9 30.4 %collective-permute-start.8 = (bf16[512,1152]{1,0:T(8,128)(2,1)}, bf16[512,1152]{1,0:T(8,128)(2,1)}, u32[]{:S(2)}, u32[]{:S(2)}) collective-permute-start(bf16[512,1152]{1,0:T(8,128)(2,1)} %collective-permute-done.7), channel_id=1, source_target_pairs={{0,4},{8,12},{16,20},{24,28},{1,5},{9,13},{17,21},{25,29},{2,6},{1... | collective-permute-start | bytes 3538952 | tf_op jit(solution)/shard_map/ppermute | solution.py:18
  225.8 8.7 %collective-permute-start.12 = (bf16[2,36,1152]{2,0,1:T(2,128)(2,1)S(1)}, bf16[2,36,1152]{2,0,1:T(2,128)(2,1)}, u32[]{:S(2)}, u32[]{:S(2)}) collective-permute-start(bf16[2,36,1152]{2,0,1:T(2,128)(2,1)S(1)} %dynamic-slice_convert_fusion.2), channel_id=1, source_target_pairs={{0,8},{4,12},{8,0},{12,4},{16,24},{20,28},{24,16},{28,20},{1,9},{5... | collective-permute-start | bytes 497672 | tf_op jit(solution)/shard_map/ppermute | solution.py:18
  235.6 0.7 copy-start.11
  236.5 6.9 %collective-permute-start.13 = (bf16[1,36,1152]{2,0,1:T(2,128)(2,1)S(1)}, bf16[1,36,1152]{2,0,1:T(2,128)(2,1)S(1)}, u32[]{:S(2)}, u32[]{:S(2)}) collective-permute-start(bf16[1,36,1152]{2,0,1:T(2,128)(2,1)S(1)} %dynamic-slice_convert_fusion.3), channel_id=1, source_target_pairs={{0,4},{4,0},{8,12},{12,8},{16,20},{20,16},{24,28},{28,24},{1,5},{5... | collective-permute-start | bytes 248840 | tf_op jit(solution)/shard_map/ppermute | solution.py:18
  236.6 6.8 %copy-start.12 = (f32[2,36,1152]{2,0,1:T(2,128)S(1)}, f32[2,36,1152]{2,0,1:T(2,128)}, u32[]{:S(2)}) copy-start(f32[2,36,1152]{2,0,1:T(2,128)} %copy-done.11) | copy-start | bytes 995332
  243.7 8.1 %collective-permute-start.14 = (f32[36,1152]{1,0:T(8,128)S(1)}, f32[36,1152]{1,0:T(8,128)S(1)}, u32[]{:S(2)}, u32[]{:S(2)}) collective-permute-start(f32[36,1152]{1,0:T(8,128)S(1)} %bitcast.67), channel_id=1, source_target_pairs={{0,2},{1,3},{2,0},{3,1},{4,6},{5,7},{6,4},{7,5},{8,10},{9,11},{10,... | collective-permute-start | bytes 497672 | tf_op jit(solution)/shard_map/ppermute | solution.py:18
  251.8 1.3 copy-start.3
  251.9 4.4 %collective-permute-start.15 = (f32[72,1152]{1,0:T(8,128)S(1)}, f32[72,1152]{1,0:T(8,128)S(1)}, u32[]{:S(2)}, u32[]{:S(2)}) collective-permute-start(f32[72,1152]{1,0:T(8,128)S(1)} %pad_maximum_fusion.1), channel_id=1, source_target_pairs={{0,1},{1,0},{2,3},{3,2},{4,5},{5,4},{6,7},{7,6},{8,9},{9,8},{10,11... | collective-permute-start | bytes 995336 | tf_op jit(solution)/shard_map/ppermute | solution.py:18

commit v2 on v1

v2 whole, which is shorter than its diff:
```python
import jax
import jax.numpy as jnp
from jax import lax
from jax.sharding import PartitionSpec as P

HOPS = 4


def shifted(value, axis, steps):
    count = lax.axis_size(axis)
    pairs = [(source, (source + steps) % count) for source in range(count)]
    return lax.ppermute(value, axis, pairs)


def swapped(value, axis, bit, senders=(0, 1)):
    count = lax.axis_size(axis)
    pairs = [(k, k ^ bit) for k in range(count) if (k // bit) % 2 in senders]
    return lax.ppermute(value, axis, pairs)


def after(value, *others):
    return lax.optimization_barrier((value, *others))[0]


def unit_rows(values):
    inverse = lax.rsqrt(jnp.sum(values * values, axis=-1, keepdims=True) + 1e-06)
    return (values * inverse, inverse)


def halved(value, axis, bit, dim):
    half = value.shape[dim] // 2
    mine = (lax.axis_index(axis) // bit) % 2
    send = lax.dynamic_slice_in_dim(value, (1 - mine) * half, half, dim).astype(jnp.bfloat16)
    keep = lax.dynamic_slice_in_dim(value, mine * half, half, dim)
    return keep + swapped(send, axis, bit).astype(jnp.float32)


def head_rows(partial, arrived):
    n_blk, n_rep = lax.axis_size("blk"), lax.axis_size("rep")
    rows, columns = partial.shape
    value = partial.reshape(n_blk, rows // n_blk, columns)
    split = []
    bit = 1
    while bit < n_rep:
        if value.shape[1] % 2 == 0:
            value = halved(value, "rep", bit, 1)
            split.append(bit)
        else:
            value = value + swapped(value, "rep", bit)
        bit *= 2
    value = after(value, arrived)
    bit = n_blk // 2
    while bit >= 1:
        value = halved(value, "blk", bit, 0)
        bit //= 2
    value = value[0] / (n_blk * n_rep)
    for bit in reversed(split):
        mine = (lax.axis_index("rep") // bit) % 2
        other = swapped(value, "rep", bit)
        first = jnp.where(mine == 0, value, other)
        second = jnp.where(mine == 0, other, value)
        value = jnp.concatenate([first, second], axis=0)
    return value


def with_ids(half, ids):
    digits = jnp.stack([ids // 256, ids % 256]).astype(half.dtype)
    digits = jnp.pad(digits, ((0, 6), (0, half.shape[1] - ids.shape[0])))
    return jnp.concatenate([half, digits], axis=0)


def split_ids(packed):
    rows = packed.shape[0] - 8
    digits = packed[rows : rows + 2, :rows].astype(jnp.float32)
    return (packed[:rows], digits[0] * 256.0 + digits[1])


def per_device(image_feats, text_feats, head, image_ids, text_ids, log_scale, bias):
    odd = lax.axis_index("blk") % 2 == 1
    scale = jnp.exp(log_scale[0])
    offset = bias[0]
    image_labels = image_ids.astype(jnp.float32)
    text_labels = text_ids.astype(jnp.float32)

    def coefficients(rows, row_labels, columns, column_labels):
        logits = (
            scale * jnp.einsum("id,jd->ij", rows, columns, preferred_element_type=jnp.float32)
            + offset
        )
        positive = (row_labels[:, None] == column_labels[None, :]).astype(jnp.float32)
        coef = (scale * (jax.nn.sigmoid(logits) - positive)).astype(jnp.bfloat16)
        return lax.optimization_barrier(coef)

    def image_part(packed):
        texts, labels = split_ids(packed)
        coef = coefficients(x_half, image_labels, texts, labels)
        return jnp.dot(coef, texts, preferred_element_type=jnp.float32)

    def text_part(packed):
        images, labels = split_ids(packed)
        coef = coefficients(y_half, text_labels, images, labels)
        return jnp.dot(coef, images, preferred_element_type=jnp.float32)

    y_full, inv_t = unit_rows(text_feats.astype(jnp.float32))
    y_half = y_full.astype(jnp.bfloat16)
    y_own = lax.optimization_barrier(with_ids(y_half, text_ids))
    y_back2 = shifted(y_own, "blk", 2)
    u_local = jnp.dot(after(image_feats, y_own), head, preferred_element_type=jnp.float32)
    x_full, inv_u = unit_rows(u_local)
    x_half = x_full.astype(jnp.bfloat16)
    x_own = with_ids(x_half, image_ids)
    own = coefficients(x_half, image_labels, y_half, text_labels)
    grad_x = jnp.dot(own, y_half, preferred_element_type=jnp.float32)
    grad_y = jnp.einsum("ij,id->jd", own, x_half, preferred_element_type=jnp.float32)
    y_back2, x_own, grad_x, grad_y = lax.optimization_barrier((y_back2, x_own, grad_x, grad_y))

    y_back4 = shifted(y_back2, "blk", 2)
    y_cross2 = swapped(y_back2, "blk", 1)
    grad_x = grad_x + image_part(y_back2)
    y_back4, y_cross2, grad_x = lax.optimization_barrier((y_back4, y_cross2, grad_x))

    x_fore2 = shifted(after(x_own, y_back4), "blk", -2)
    y_cross4 = swapped(jnp.where(odd, y_back4, y_own), "blk", 1)
    grad_x = grad_x + image_part(y_cross2)
    grad_x = grad_x + image_part(y_back4)
    x_fore2, y_cross4, grad_x = lax.optimization_barrier((x_fore2, y_cross4, grad_x))

    x_fore4 = shifted(x_fore2, "blk", -2)
    x_cross2 = swapped(x_fore2, "blk", 1)
    grad_x = lax.optimization_barrier(grad_x + image_part(y_cross4))
    grad_u = (inv_u * (grad_x - x_full * jnp.sum(x_full * grad_x, axis=1, keepdims=True))).astype(
        jnp.bfloat16
    )
    partial = jnp.einsum("ie,id->ed", image_feats, grad_u, preferred_element_type=jnp.float32)
    grad_image = jnp.einsum("id,ed->ie", grad_u, head, preferred_element_type=jnp.float32).astype(
        jnp.bfloat16
    )
    grad_y = grad_y + text_part(x_fore2)

    x_cross4 = swapped(jnp.where(odd, x_own, x_fore4), "blk", 1)
    grad_head = head_rows(partial, x_fore4)
    grad_y = grad_y + text_part(x_cross2)
    grad_y = grad_y + text_part(x_fore4)
    grad_y = lax.optimization_barrier(grad_y + text_part(x_cross4))
    grad_text = (
        inv_t * (grad_y - y_full * jnp.sum(y_full * grad_y, axis=1, keepdims=True))
    ).astype(jnp.bfloat16)
    return (grad_image, grad_text, grad_head)


def solution(mesh):
    placed = (
        P(("blk", "rep"), None),
        P(("blk", "rep"), None),
        P(),
        P(("blk", "rep")),
        P(("blk", "rep")),
        P(),
        P(),
    )
    return jax.shard_map(
        per_device,
        mesh=mesh,
        in_specs=placed,
        out_specs=(P(("blk", "rep"), None), P(("blk", "rep"), None), P("blk", None)),
        check_vma=False,
    )
```

time: 258 us -> 170 us (0.66)
  blocking collectives: 68 us -> 0 us
  matrix products: 65 us -> 36.3 us
  waiting for transfers between devices: 73.7 us -> 96.7 us
  local copies, waits for them, and re-layouts: 11.8 us -> 4.79 us
  other arithmetic: 16.1 us -> 11 us
  starting transfers between devices: 20.3 us -> 17.7 us
    all_gather x1 -> x0, blocking collectives: 68 us -> none  [per_device(): ids = lax.all_gather(jnp.stack([image_ids, text_ids]), 'blk')]
    ppermute x12 -> x11, waiting for transfers between devices: 12.1 us -> 46.3 us  [swapped(): return lax.ppermute(value, axis, pairs)]
    dot_general x4, matrix products: 24.6 us -> 7.48 us  [image_part(): return jnp.dot(coef, texts, preferred_element_type=jnp.float32)]
    dot_general x6 -> x14, matrix products: 30.9 us -> 19.4 us  [the longest x9 14 us: coefficients(): jnp.einsum('id,jd->ij', rows, columns, preferred_element_type=jnp.float32)]
    ppermute x4, waiting for transfers between devices: 61.6 us -> 50.4 us  [shifted(): return lax.ppermute(value, axis, pairs)]
    unnamed x34 -> x38, local copies, waits for them, and re-layouts: 8.32 us -> 3.91 us
    add x4, other arithmetic: 4.92 us -> 1.12 us  [halved(): return keep + swapped(send, axis, bit).astype(jnp.float32)]
    ppermute x12 -> x11, starting transfers between devices: 12.6 us -> 10 us  [swapped(): return lax.ppermute(value, axis, pairs)]
  transfers between devices with their start and end apart: 16 -> 15, of which waited for: 6 -> 12; matrix products, arithmetic and copies ran while one was open for 25% -> 26% of each run, Pallas kernels for 0% -> 0%
where the time goes in v2:
time: 170 us; the launch traced here: 169 us
  waiting for transfers between devices  96.7 us (57%)
  matrix products  36.3 us (21%)
  starting transfers between devices  17.7 us (10%)
  other arithmetic  11 us (6%)
  local copies, waits for them, and re-layouts  4.79 us (3%)
  between operations  2.62 us (2%)
    ppermute x4, waiting for transfers between devices, shifted(): return lax.ppermute(value, axis, pairs)  50.4 us
    ppermute x11, waiting for transfers between devices, swapped(): return lax.ppermute(value, axis, pairs)  46.3 us
    dot_general x9, matrix products, coefficients(): jnp.einsum('id,jd->ij', rows, columns, preferred_element_type=jnp.float32)  14 us
    ppermute x11, starting transfers between devices, swapped(): return lax.ppermute(value, axis, pairs)  10 us
    ppermute x4, starting transfers between devices, shifted(): return lax.ppermute(value, axis, pairs)  7.65 us
    dot_general x4, matrix products, image_part(): return jnp.dot(coef, texts, preferred_element_type=jnp.float32)  7.48 us
    unnamed x38, local copies, waits for them, and re-layouts  3.91 us
    dot_general x4, matrix products, text_part(): return jnp.dot(coef, images, preferred_element_type=jnp.float32)  3.54 us
  transfers between devices with their start and end apart: 15, of which 12 were waited for; matrix products, arithmetic and copies ran while one was open for 26% of the time, Pallas kernels for 0%

profile of v2, /device:TPU:0, one launch (start us, length us, event | category | flops | bytes accessed | tf_op | source)
XLA Modules:
  0.0 169.0 jit_solution(8551589895086731287)
XLA Ops:
  0.7 1.7 %fusion.7 = f32[512]{0:T(512)S(1)} fusion(bf16[512,1152]{1,0:T(8,128)(2,1)} %param.8), kind=kLoop, calls=%fused_computation.12 | loop fusion | flops 1768960 | bytes 1181696 | tf_op jit(solution)/shard_map/reduce_sum | solution.py:26
  3.3 3.1 %collective-permute-start = (bf16[520,1152]{1,0:T(8,128)(2,1)S(1)}, bf16[520,1152]{1,0:T(8,128)(2,1)}, u32[]{:S(2)}, u32[]{:S(2)}) collective-permute-start(bf16[520,1152]{1,0:T(8,128)(2,1)S(1)} %pad_maximum_fusion), channel_id=1, source_target_pairs={{0,8},{4,12},{8,16},{12,20},{16,24},{20,28},{24,0},{28,4},{1,9},{5... | collective-permute-start | bytes 3594248 | tf_op jit(solution)/shard_map/ppermute | solution.py:12
  6.4 1.9 %multiply_reduce_fusion.1 = (f32[512]{0:T(512)S(1)}, f32[512,1152]{1,0:T(8,128)S(1)}) fusion(bf16[512,1152]{1,0:T(8,128)(2,1)S(1)} %copy-done.14, bf16[1152,1152]{1,0:T(8,128)(2,1)S(1)} %copy-done), kind=kOutput, calls=%fused_computation.17 | convolution fusion | flops 1360133632 | bytes 6195200 | tf_op jit(solution)/shard_map/dot_general | solution.py:108
  12.3 2.3 %fusion.128 = f32[512,1152]{1,0:T(8,128)} fusion(bf16[512,512]{1,0:T(8,128)(2,1)S(1)} %fusion.71, bf16[512,1152]{1,0:T(8,128)(2,1)S(1)} %multiply_convert_fusion.1), kind=kOutput, calls=%fused_computation.207 | convolution fusion | flops 603979776 | bytes 4063232 | tf_op jit(solution)/shard_map/ij,id->jd/dot_general | solution.py:114
  14.6 2.3 %fusion.127 = f32[512,1152]{1,0:T(8,128)} fusion(bf16[512,512]{1,0:T(8,128)(2,1)S(1)} %fusion.71, bf16[512,1152]{1,0:T(8,128)(2,1)S(1)} %fusion.2), kind=kOutput, calls=%fused_computation.206 | convolution fusion | flops 603979776 | bytes 4063232 | tf_op jit(solution)/shard_map/dot_general | solution.py:113
  16.9 17.9 %collective-permute-done = bf16[520,1152]{1,0:T(8,128)(2,1)} collective-permute-done((bf16[520,1152]{1,0:T(8,128)(2,1)S(1)}, bf16[520,1152]{1,0:T(8,128)(2,1)}, u32[]{:S(2)}, u32[]{:S(2)}) %collective-permute-start) | collective-permute-done | bytes 1198112 | tf_op jit(solution)/shard_map/ppermute | solution.py:12
  34.8 1.5 collective-permute-start.2
  37.1 2.7 %fusion.72 = bf16[512,512]{1,0:T(8,128)(2,1)S(1)} fusion(bf16[512,1152]{1,0:T(8,128)(2,1)} %copy-done.7, bf16[520,1152]{1,0:T(8,128)(2,1)} %collective-permute-done, f32[512]{0:T(512)S(1)} %bitcast.63, f32[]{:T(128)} %bitcast.56, f32[]{:T(128)} %bitcast, f32[512]{0:T(512)S(1)} %get-tuple-element.33), kind=kOutput, calls=%fused_computation.94 | convolution fusion | flops 606601216 | bytes 2888704 | tf_op jit(solution)/shard_map/id,jd->ij/dot_general | solution.py:87
  39.8 2.3 %fusion.105 = f32[512,1152]{1,0:T(8,128)S(1)} fusion(bf16[512,512]{1,0:T(8,128)(2,1)S(1)} %fusion.72, bf16[520,1152]{1,0:T(8,128)(2,1)} %collective-permute-done), kind=kOutput, calls=%fused_computation.127 | convolution fusion | flops 603979776 | bytes 4063232 | tf_op jit(solution)/shard_map/dot_general | solution.py:97
  42.4 22.1 %collective-permute-done.1 = bf16[520,1152]{1,0:T(8,128)(2,1)} collective-permute-done((bf16[520,1152]{1,0:T(8,128)(2,1)}, bf16[520,1152]{1,0:T(8,128)(2,1)}, u32[]{:S(2)}, u32[]{:S(2)}) %collective-permute-start.1) | collective-permute-done | bytes 1198112 | tf_op jit(solution)/shard_map/ppermute | solution.py:12
  65.5 2.8 %collective-permute-start.4 = (bf16[520,1152]{1,0:T(8,128)(2,1)S(1)}, bf16[520,1152]{1,0:T(8,128)(2,1)S(1)}, u32[]{:S(2)}, u32[]{:S(2)}) collective-permute-start(bf16[520,1152]{1,0:T(8,128)(2,1)S(1)} %broadcast_select_fusion.1), channel_id=1, source_target_pairs={{0,4},{4,0},{8,12},{12,8},{16,20},{20,16},{24,28},{28,24},{1,5},{5... | collective-permute-start | bytes 3594248 | tf_op jit(solution)/shard_map/ppermute | solution.py:18
  68.2 1.7 %collective-permute-start.3 = (bf16[520,1152]{1,0:T(8,128)(2,1)S(1)}, bf16[520,1152]{1,0:T(8,128)(2,1)S(1)}, u32[]{:S(2)}, u32[]{:S(2)}) collective-permute-start(bf16[520,1152]{1,0:T(8,128)(2,1)S(1)} %copy-done.11), channel_id=1, source_target_pairs={{0,24},{4,28},{8,0},{12,4},{16,8},{20,12},{24,16},{28,20},{1,25},{... | collective-permute-start | bytes 3594248 | tf_op jit(solution)/shard_map/ppermute | solution.py:12
  70.0 2.4 %fusion.74 = bf16[512,512]{1,0:T(8,128)(2,1)S(1)} fusion(bf16[512,1152]{1,0:T(8,128)(2,1)S(1)} %copy-done.8, bf16[520,1152]{1,0:T(8,128)(2,1)} %collective-permute-done.1, f32[512]{0:T(512)S(1)} %bitcast.60, f32[]{:T(128)} %bitcast.54, f32[]{:T(128)} %bitcast, f32[512]{0:T(512)S(1)} %get-tuple-element.33), kind=kOutput, calls=%fused_computation.96 | convolution fusion | flops 606601216 | bytes 2888704 | tf_op jit(solution)/shard_map/id,jd->ij/dot_general | solution.py:87
  72.4 2.4 %fusion.73 = bf16[512,512]{1,0:T(8,128)(2,1)S(1)} fusion(bf16[512,1152]{1,0:T(8,128)(2,1)S(1)} %copy-done.8, bf16[520,1152]{1,0:T(8,128)(2,1)} %collective-permute-done.2, f32[512]{0:T(512)S(1)} %bitcast.64, f32[]{:T(128)} %bitcast.55, f32[]{:T(128)} %bitcast, f32[512]{0:T(512)S(1)} %get-tuple-element.33), kind=kOutput, calls=%fused_computation.95 | convolution fusion | flops 606601216 | bytes 2888704 | tf_op jit(solution)/shard_map/id,jd->ij/dot_general | solution.py:87
  74.7 2.1 %fusion.102 = f32[512,1152]{1,0:T(8,128)S(1)} fusion(bf16[512,512]{1,0:T(8,128)(2,1)S(1)} %fusion.73, bf16[520,1152]{1,0:T(8,128)(2,1)} %collective-permute-done.2), kind=kOutput, calls=%fused_computation.124 | convolution fusion | flops 603979776 | bytes 4063232 | tf_op jit(solution)/shard_map/dot_general | solution.py:97
  76.9 2.2 %add_add_fusion.1 = f32[512,1152]{1,0:T(8,128)S(1)} fusion(f32[512,1152]{1,0:T(8,128)S(1)} %add.233, f32[512,1152]{1,0:T(8,128)S(1)} %fusion.102, bf16[512,512]{1,0:T(8,128)(2,1)S(1)} %fusion.74, bf16[520,1152]{1,0:T(8,128)(2,1)} %collective-permute-done.1), kind=kOutput, calls=%fused_computation.16 | convolution fusion | flops 605159424 | bytes 8781824 | tf_op jit(solution)/shard_map/dot_general | solution.py:97
  79.1 13.8 %collective-permute-done.4 = bf16[520,1152]{1,0:T(8,128)(2,1)S(1)} collective-permute-done((bf16[520,1152]{1,0:T(8,128)(2,1)S(1)}, bf16[520,1152]{1,0:T(8,128)(2,1)S(1)}, u32[]{:S(2)}, u32[]{:S(2)}) %collective-permute-start.4) | collective-permute-done | bytes 1198112 | tf_op jit(solution)/shard_map/ppermute | solution.py:18
  92.9 1.9 %collective-permute-done.3 = bf16[520,1152]{1,0:T(8,128)(2,1)S(1)} collective-permute-done((bf16[520,1152]{1,0:T(8,128)(2,1)S(1)}, bf16[520,1152]{1,0:T(8,128)(2,1)S(1)}, u32[]{:S(2)}, u32[]{:S(2)}) %collective-permute-start.3) | collective-permute-done | bytes 1198112 | tf_op jit(solution)/shard_map/ppermute | solution.py:12
  94.8 2.8 %collective-permute-start.6 = (bf16[520,1152]{1,0:T(8,128)(2,1)S(1)}, bf16[520,1152]{1,0:T(8,128)(2,1)S(1)}, u32[]{:S(2)}, u32[]{:S(2)}) collective-permute-start(bf16[520,1152]{1,0:T(8,128)(2,1)S(1)} %collective-permute-done.3), channel_id=1, source_target_pairs={{0,24},{4,28},{8,0},{12,4},{16,8},{20,12},{24,16},{28,20},{1,25},{... | collective-permute-start | bytes 3594248 | tf_op jit(solution)/shard_map/ppermute | solution.py:12
  100.2 1.4 copy-done.2
  103.2 1.8 %fusion.129 = f32[1152,1152]{0,1:T(8,128)S(1)} fusion(bf16[512,1152]{1,0:T(8,128)(2,1)S(1)} %multiply_convert_fusion, bf16[512,1152]{1,0:T(8,128)(2,1)S(1)} %copy-done.15), kind=kOutput, calls=%fused_computation.208 | convolution fusion | flops 1358954496 | bytes 7667712 | tf_op jit(solution)/shard_map/ie,id->ed/dot_general | solution.py:134
  108.6 2.9 %convolution_convert_fusion = bf16[512,1152]{1,0:T(8,128)(2,1)} fusion(bf16[512,1152]{1,0:T(8,128)(2,1)S(1)} %multiply_convert_fusion, bf16[1152,1152]{1,0:T(8,128)(2,1)S(1)} %copy-done), kind=kOutput, calls=%fused_computation | convolution fusion | flops 1359544320 | bytes 5013504 | tf_op jit(solution)/shard_map/id,ed->ie/dot_general | solution.py:135
  111.5 8.5 %collective-permute-done.6 = bf16[520,1152]{1,0:T(8,128)(2,1)S(1)} collective-permute-done((bf16[520,1152]{1,0:T(8,128)(2,1)S(1)}, bf16[520,1152]{1,0:T(8,128)(2,1)S(1)}, u32[]{:S(2)}, u32[]{:S(2)}) %collective-permute-start.6) | collective-permute-done | bytes 1198112 | tf_op jit(solution)/shard_map/ppermute | solution.py:12
  120.9 4.7 %collective-permute-done.5 = bf16[520,1152]{1,0:T(8,128)(2,1)S(1)} collective-permute-done((bf16[520,1152]{1,0:T(8,128)(2,1)S(1)}, bf16[520,1152]{1,0:T(8,128)(2,1)S(1)}, u32[]{:S(2)}, u32[]{:S(2)}) %collective-permute-start.5) | collective-permute-done | bytes 1198112 | tf_op jit(solution)/shard_map/ppermute | solution.py:18
  127.3 1.6 collective-permute-start.9
  129.9 8.1 %collective-permute-done.9 = bf16[8,36,1152]{2,0,1:T(8,128)(2,1)S(1)} collective-permute-done((bf16[8,36,1152]{2,0,1:T(8,128)(2,1)S(1)}, bf16[8,36,1152]{2,0,1:T(8,128)(2,1)S(1)}, u32[]{:S(2)}, u32[]{:S(2)}) %collective-permute-start.9) | collective-permute-done | bytes 663584 | tf_op jit(solution)/shard_map/ppermute | solution.py:18
  140.1 8.5 %collective-permute-done.10 = bf16[4,36,1152]{2,0,1:T(4,128)(2,1)S(1)} collective-permute-done((bf16[4,36,1152]{2,0,1:T(4,128)(2,1)S(1)}, bf16[4,36,1152]{2,0,1:T(4,128)(2,1)S(1)}, u32[]{:S(2)}, u32[]{:S(2)}) %collective-permute-start.10) | collective-permute-done | bytes 331808 | tf_op jit(solution)/shard_map/ppermute | solution.py:18
  150.4 4.2 %collective-permute-done.11 = bf16[2,36,1152]{2,0,1:T(2,128)(2,1)S(1)} collective-permute-done((bf16[2,36,1152]{2,0,1:T(2,128)(2,1)S(1)}, bf16[2,36,1152]{2,0,1:T(2,128)(2,1)S(1)}, u32[]{:S(2)}, u32[]{:S(2)}) %collective-permute-start.11) | collective-permute-done | bytes 165920 | tf_op jit(solution)/shard_map/ppermute | solution.py:18
  157.1 3.3 %collective-permute-done.12 = bf16[1,36,1152]{2,0,1:T(2,128)(2,1)S(1)} collective-permute-done((bf16[1,36,1152]{2,0,1:T(2,128)(2,1)S(1)}, bf16[1,36,1152]{2,0,1:T(2,128)(2,1)S(1)}, u32[]{:S(2)}, u32[]{:S(2)}) %collective-permute-start.12) | collective-permute-done | bytes 82976 | tf_op jit(solution)/shard_map/ppermute | solution.py:18
  160.7 1.6 collective-permute-start.13
  162.7 3.6 %collective-permute-done.13 = f32[36,1152]{1,0:T(8,128)S(1)} collective-permute-done((f32[36,1152]{1,0:T(8,128)S(1)}, f32[36,1152]{1,0:T(8,128)S(1)}, u32[]{:S(2)}, u32[]{:S(2)}) %collective-permute-start.13) | collective-permute-done | bytes 165920 | tf_op jit(solution)/shard_map/ppermute | solution.py:18
  166.4 1.5 fusion.6
  (111 shorter events, 24.8 us)
Async XLA Ops:
  0.6 5.7 %copy-start = (bf16[1152,1152]{1,0:T(8,128)(2,1)S(1)}, bf16[1152,1152]{1,0:T(8,128)(2,1)}, u32[]{:S(2)}) copy-start(bf16[1152,1152]{1,0:T(8,128)(2,1)} %param.9) | copy-start | bytes 7962628
  0.6 1.8 %copy-start.3 = (bf16[512,1152]{1,0:T(8,128)(2,1)S(1)}, bf16[512,1152]{1,0:T(8,128)(2,1)}, u32[]{:S(2)}) copy-start(bf16[512,1152]{1,0:T(8,128)(2,1)} %param.8) | copy-start | bytes 3538948
  3.1 11.5 %copy-start.9 = (bf16[512,1152]{1,0:T(8,128)(2,1)}, bf16[512,1152]{1,0:T(8,128)(2,1)S(1)}, u32[]{:S(2)}) copy-start(bf16[512,1152]{1,0:T(8,128)(2,1)S(1)} %fusion.2) | copy-start | bytes 3538948
  3.1 3.2 %copy-start.14 = (bf16[512,1152]{1,0:T(8,128)(2,1)S(1)}, bf16[512,1152]{1,0:T(8,128)(2,1)}, u32[]{:S(2)}) copy-start(bf16[512,1152]{1,0:T(8,128)(2,1)} %param.7) | copy-start | bytes 3538948
  3.3 5.1 %copy-start.12 = (bf16[520,1152]{1,0:T(8,128)(2,1)}, bf16[520,1152]{1,0:T(8,128)(2,1)S(1)}, u32[]{:S(2)}) copy-start(bf16[520,1152]{1,0:T(8,128)(2,1)S(1)} %pad_maximum_fusion) | copy-start | bytes 3594244
  3.3 6.5 %copy-start.17 = (s32[512]{0:T(512)S(1)}, s32[512]{0:T(512)}, u32[]{:S(2)}) copy-start(s32[512]{0:T(512)} %param.10) | copy-start | bytes 6148
  3.3 31.6 %collective-permute-start = (bf16[520,1152]{1,0:T(8,128)(2,1)S(1)}, bf16[520,1152]{1,0:T(8,128)(2,1)}, u32[]{:S(2)}, u32[]{:S(2)}) collective-permute-start(bf16[520,1152]{1,0:T(8,128)(2,1)S(1)} %pad_maximum_fusion), channel_id=1, source_target_pairs={{0,8},{4,12},{8,16},{12,20},{16,24},{20,28},{24,0},{28,4},{1,9},{5... | collective-permute-start | bytes 3594248 | tf_op jit(solution)/shard_map/ppermute | solution.py:12
  8.3 1.7 copy-start.1
  10.0 2.3 %copy-start.7 = (bf16[512,1152]{1,0:T(8,128)(2,1)}, bf16[512,1152]{1,0:T(8,128)(2,1)S(1)}, u32[]{:S(2)}) copy-start(bf16[512,1152]{1,0:T(8,128)(2,1)S(1)} %multiply_convert_fusion.1) | copy-start | bytes 3538948
  34.8 29.7 %collective-permute-start.1 = (bf16[520,1152]{1,0:T(8,128)(2,1)}, bf16[520,1152]{1,0:T(8,128)(2,1)}, u32[]{:S(2)}, u32[]{:S(2)}) collective-permute-start(bf16[520,1152]{1,0:T(8,128)(2,1)} %collective-permute-done), channel_id=1, source_target_pairs={{0,8},{4,12},{8,16},{12,20},{16,24},{20,28},{24,0},{28,4},{1,9},{5... | collective-permute-start | bytes 3594248 | tf_op jit(solution)/shard_map/ppermute | solution.py:12
  34.8 29.7 %collective-permute-start.2 = (bf16[520,1152]{1,0:T(8,128)(2,1)}, bf16[520,1152]{1,0:T(8,128)(2,1)}, u32[]{:S(2)}, u32[]{:S(2)}) collective-permute-start(bf16[520,1152]{1,0:T(8,128)(2,1)} %collective-permute-done), channel_id=1, source_target_pairs={{0,4},{4,0},{8,12},{12,8},{16,20},{20,16},{24,28},{28,24},{1,5},{5... | collective-permute-start | bytes 3594248 | tf_op jit(solution)/shard_map/ppermute | solution.py:18
  39.8 2.3 %copy-start.6 = (f32[512,1152]{1,0:T(8,128)S(1)}, f32[512,1152]{1,0:T(8,128)}, u32[]{:S(2)}) copy-start(f32[512,1152]{1,0:T(8,128)} %fusion.127) | copy-start | bytes 7077892
  42.1 23.1 %copy-start.13 = (bf16[520,1152]{1,0:T(8,128)(2,1)S(1)}, bf16[520,1152]{1,0:T(8,128)(2,1)}, u32[]{:S(2)}) copy-start(bf16[520,1152]{1,0:T(8,128)(2,1)} %copy-done.12) | copy-start | bytes 3594244
  65.3 3.0 %copy-start.11 = (bf16[520,1152]{1,0:T(8,128)(2,1)S(1)}, bf16[520,1152]{1,0:T(8,128)(2,1)}, u32[]{:S(2)}) copy-start(bf16[520,1152]{1,0:T(8,128)(2,1)} %pad_maximum_fusion.1) | copy-start | bytes 3594244
  65.3 4.7 %copy-start.8 = (bf16[512,1152]{1,0:T(8,128)(2,1)S(1)}, bf16[512,1152]{1,0:T(8,128)(2,1)}, u32[]{:S(2)}) copy-start(bf16[512,1152]{1,0:T(8,128)(2,1)} %copy-done.7) | copy-start | bytes 3538948
  65.5 27.4 %collective-permute-start.4 = (bf16[520,1152]{1,0:T(8,128)(2,1)S(1)}, bf16[520,1152]{1,0:T(8,128)(2,1)S(1)}, u32[]{:S(2)}, u32[]{:S(2)}) collective-permute-start(bf16[520,1152]{1,0:T(8,128)(2,1)S(1)} %broadcast_select_fusion.1), channel_id=1, source_target_pairs={{0,4},{4,0},{8,12},{12,8},{16,20},{20,16},{24,28},{28,24},{1,5},{5... | collective-permute-start | bytes 3594248 | tf_op jit(solution)/shard_map/ppermute | solution.py:18
  68.2 26.5 %collective-permute-start.3 = (bf16[520,1152]{1,0:T(8,128)(2,1)S(1)}, bf16[520,1152]{1,0:T(8,128)(2,1)S(1)}, u32[]{:S(2)}, u32[]{:S(2)}) collective-permute-start(bf16[520,1152]{1,0:T(8,128)(2,1)S(1)} %copy-done.11), channel_id=1, source_target_pairs={{0,24},{4,28},{8,0},{12,4},{16,8},{20,12},{24,16},{28,20},{1,25},{... | collective-permute-start | bytes 3594248 | tf_op jit(solution)/shard_map/ppermute | solution.py:12
  94.8 25.3 %collective-permute-start.6 = (bf16[520,1152]{1,0:T(8,128)(2,1)S(1)}, bf16[520,1152]{1,0:T(8,128)(2,1)S(1)}, u32[]{:S(2)}, u32[]{:S(2)}) collective-permute-start(bf16[520,1152]{1,0:T(8,128)(2,1)S(1)} %collective-permute-done.3), channel_id=1, source_target_pairs={{0,24},{4,28},{8,0},{12,4},{16,8},{20,12},{24,16},{28,20},{1,25},{... | collective-permute-start | bytes 3594248 | tf_op jit(solution)/shard_map/ppermute | solution.py:12
  97.6 27.9 %collective-permute-start.5 = (bf16[520,1152]{1,0:T(8,128)(2,1)S(1)}, bf16[520,1152]{1,0:T(8,128)(2,1)S(1)}, u32[]{:S(2)}, u32[]{:S(2)}) collective-permute-start(bf16[520,1152]{1,0:T(8,128)(2,1)S(1)} %collective-permute-done.3), channel_id=1, source_target_pairs={{0,4},{4,0},{8,12},{12,8},{16,20},{20,16},{24,28},{28,24},{1,5},{5... | collective-permute-start | bytes 3594248 | tf_op jit(solution)/shard_map/ppermute | solution.py:18
  99.9 1.7 copy-start.2
  102.0 1.3 copy-start.15
  105.2 1.3 copy-start.10
  105.4 21.2 %collective-permute-start.8 = (bf16[8,72,1152]{2,0,1:T(8,128)(2,1)S(1)}, bf16[8,72,1152]{2,0,1:T(8,128)(2,1)S(1)}, u32[]{:S(2)}, u32[]{:S(2)}) collective-permute-start(bf16[8,72,1152]{2,0,1:T(8,128)(2,1)S(1)} %copy.22), channel_id=1, source_target_pairs={{0,1},{1,0},{2,3},{3,2},{4,5},{5,4},{6,7},{7,6},{8,9},{9,8},{10,11... | collective-permute-start | bytes 3981320 | tf_op jit(solution)/shard_map/ppermute | solution.py:18
  120.2 29.1 %collective-permute-start.7 = (bf16[520,1152]{1,0:T(8,128)(2,1)S(1)}, bf16[520,1152]{1,0:T(8,128)(2,1)S(1)}, u32[]{:S(2)}, u32[]{:S(2)}) collective-permute-start(bf16[520,1152]{1,0:T(8,128)(2,1)S(1)} %broadcast_select_fusion), channel_id=1, source_target_pairs={{0,4},{4,0},{8,12},{12,8},{16,20},{20,16},{24,28},{28,24},{1,5},{5... | collective-permute-start | bytes 3594248 | tf_op jit(solution)/shard_map/ppermute | solution.py:18
  127.3 10.7 %collective-permute-start.9 = (bf16[8,36,1152]{2,0,1:T(8,128)(2,1)S(1)}, bf16[8,36,1152]{2,0,1:T(8,128)(2,1)S(1)}, u32[]{:S(2)}, u32[]{:S(2)}) collective-permute-start(bf16[8,36,1152]{2,0,1:T(8,128)(2,1)S(1)} %dynamic-slice_convert_fusion), channel_id=1, source_target_pairs={{0,2},{1,3},{2,0},{3,1},{4,6},{5,7},{6,4},{7,5},{8,10},{9,11},{10,... | collective-permute-start | bytes 1990664 | tf_op jit(solution)/shard_map/ppermute | solution.py:18
  138.3 10.3 %collective-permute-start.10 = (bf16[4,36,1152]{2,0,1:T(4,128)(2,1)S(1)}, bf16[4,36,1152]{2,0,1:T(4,128)(2,1)S(1)}, u32[]{:S(2)}, u32[]{:S(2)}) collective-permute-start(bf16[4,36,1152]{2,0,1:T(4,128)(2,1)S(1)} %dynamic-slice_convert_fusion.1), channel_id=1, source_target_pairs={{0,16},{4,20},{8,24},{12,28},{16,0},{20,4},{24,8},{28,12},{1,17},{... | collective-permute-start | bytes 995336 | tf_op jit(solution)/shard_map/ppermute | solution.py:18
  149.0 5.6 %collective-permute-start.11 = (bf16[2,36,1152]{2,0,1:T(2,128)(2,1)S(1)}, bf16[2,36,1152]{2,0,1:T(2,128)(2,1)S(1)}, u32[]{:S(2)}, u32[]{:S(2)}) collective-permute-start(bf16[2,36,1152]{2,0,1:T(2,128)(2,1)S(1)} %dynamic-slice_convert_fusion.2), channel_id=1, source_target_pairs={{0,8},{4,12},{8,0},{12,4},{16,24},{20,28},{24,16},{28,20},{1,9},{5... | collective-permute-start | bytes 497672 | tf_op jit(solution)/shard_map/ppermute | solution.py:18
  149.3 6.8 %copy-start.5 = (f32[512,1152]{1,0:T(8,128)S(1)}, f32[512,1152]{1,0:T(8,128)}, u32[]{:S(2)}) copy-start(f32[512,1152]{1,0:T(8,128)} %fusion.128) | copy-start | bytes 7077892
  155.0 5.4 %collective-permute-start.12 = (bf16[1,36,1152]{2,0,1:T(2,128)(2,1)S(1)}, bf16[1,36,1152]{2,0,1:T(2,128)(2,1)S(1)}, u32[]{:S(2)}, u32[]{:S(2)}) collective-permute-start(bf16[1,36,1152]{2,0,1:T(2,128)(2,1)S(1)} %dynamic-slice_convert_fusion.3), channel_id=1, source_target_pairs={{0,4},{4,0},{8,12},{12,8},{16,20},{20,16},{24,28},{28,24},{1,5},{5... | collective-permute-start | bytes 248840 | tf_op jit(solution)/shard_map/ppermute | solution.py:18
  156.1 6.2 %copy-start.4 = (bf16[512,1152]{1,0:T(8,128)(2,1)S(1)}, bf16[512,1152]{1,0:T(8,128)(2,1)}, u32[]{:S(2)}) copy-start(bf16[512,1152]{1,0:T(8,128)(2,1)} %param.8) | copy-start | bytes 3538948
  160.7 5.6 %collective-permute-start.13 = (f32[36,1152]{1,0:T(8,128)S(1)}, f32[36,1152]{1,0:T(8,128)S(1)}, u32[]{:S(2)}, u32[]{:S(2)}) collective-permute-start(f32[36,1152]{1,0:T(8,128)S(1)} %bitcast.59), channel_id=1, source_target_pairs={{0,2},{1,3},{2,0},{3,1},{4,6},{5,7},{6,4},{7,5},{8,10},{9,11},{10,... | collective-permute-start | bytes 497672 | tf_op jit(solution)/shard_map/ppermute | solution.py:18
  166.4 1.7 %collective-permute-start.14 = (f32[72,1152]{1,0:T(8,128)S(1)}, f32[72,1152]{1,0:T(8,128)S(1)}, u32[]{:S(2)}, u32[]{:S(2)}) collective-permute-start(f32[72,1152]{1,0:T(8,128)S(1)} %pad_maximum_fusion.3), channel_id=1, source_target_pairs={{0,1},{1,0},{2,3},{3,2},{4,5},{5,4},{6,7},{7,6},{8,9},{9,8},{10,11... | collective-permute-start | bytes 995336 | tf_op jit(solution)/shard_map/ppermute | solution.py:18
  (1 other events, 0.7 us)

commit v3 on v2

--- a/solution.py
+++ b/solution.py
@@ -35,25 +35,40 @@
     return keep + swapped(send, axis, bit).astype(jnp.float32)
 
 
-def head_rows(partial, arrived):
+def head_over_rep(partial):
     n_blk, n_rep = lax.axis_size("blk"), lax.axis_size("rep")
     rows, columns = partial.shape
     value = partial.reshape(n_blk, rows // n_blk, columns)
-    split = []
-    bit = 1
-    while bit < n_rep:
-        if value.shape[1] % 2 == 0:
-            value = halved(value, "rep", bit, 1)
-            split.append(bit)
-        else:
-            value = value + swapped(value, "rep", bit)
-        bit *= 2
-    value = after(value, arrived)
-    bit = n_blk // 2
-    while bit >= 1:
-        value = halved(value, "blk", bit, 0)
-        bit //= 2
-    value = value[0] / (n_blk * n_rep)
+    bits = [1 << place for place in range(n_rep.bit_length() - 1)]
+    if value.shape[1] % n_rep:
+        split = []
+        for bit in bits:
+            if value.shape[1] % 2 == 0:
+                value = halved(value, "rep", bit, 1)
+                split.append(bit)
+            else:
+                value = value + swapped(value, "rep", bit)
+        return (value, split)
+    share = value.shape[1] // n_rep
+    me = lax.axis_index("rep")
+    mine = sum(((me // bit) % 2) * (n_rep // 2 // bit) for bit in bits)
+    total = lax.dynamic_slice_in_dim(value, mine * share, share, 1)
+    for other in range(n_rep - 1, 0, -1):
+        flips = sum(((other // bit) % 2) * (n_rep // 2 // bit) for bit in bits)
+        send = lax.dynamic_slice_in_dim(value, (mine ^ flips) * share, share, 1)
+        pairs = [(k, k ^ other) for k in range(n_rep)]
+        total = total + lax.ppermute(send.astype(jnp.bfloat16), "rep", pairs).astype(jnp.float32)
+    return (total, bits)
+
+
+def head_over_blk(value, split, arrived):
+    n_blk, n_rep = lax.axis_size("blk"), lax.axis_size("rep")
+    share = value.shape[1:]
+    n_bits = n_blk.bit_length() - 1
+    value = value.reshape((2,) * n_bits + share)
+    for place in list(range(1, n_bits)) + [0]:
+        value = halved(value, "blk", 1 << place, n_bits - 1 - place)
+    value = after(value.reshape(share) / (n_blk * n_rep), arrived)
     for bit in reversed(split):
         mine = (lax.axis_index("rep") // bit) % 2
         other = swapped(value, "rep", bit)
@@ -132,13 +147,16 @@
         jnp.bfloat16
     )
     partial = jnp.einsum("ie,id->ed", image_feats, grad_u, preferred_element_type=jnp.float32)
+    over_rep, split = head_over_rep(partial)
     grad_image = jnp.einsum("id,ed->ie", grad_u, head, preferred_element_type=jnp.float32).astype(
         jnp.bfloat16
     )
     grad_y = grad_y + text_part(x_fore2)
 
+    x_fore4, x_cross2, over_rep = lax.optimization_barrier((x_fore4, x_cross2, over_rep))
+
     x_cross4 = swapped(jnp.where(odd, x_own, x_fore4), "blk", 1)
-    grad_head = head_rows(partial, x_fore4)
+    grad_head = head_over_blk(over_rep, split, x_cross4)
     grad_y = grad_y + text_part(x_cross2)
     grad_y = grad_y + text_part(x_fore4)
     grad_y = lax.optimization_barrier(grad_y + text_part(x_cross4))

time: 170 us -> 178 us (1.047)
  waiting for transfers between devices: 96.7 us -> 105 us
    ppermute x0 -> x3, waiting for transfers between devices: none -> 24.3 us  [head_over_rep(): lax.ppermute(send.astype(jnp.bfloat16), 'rep', pairs).astype(jnp.float32)]
    ppermute x4, waiting for transfers between devices: 50.4 us -> 41.9 us  [shifted(): return lax.ppermute(value, axis, pairs)]
    ppermute x11 -> x9, waiting for transfers between devices: 46.3 us -> 38.5 us  [swapped(): return lax.ppermute(value, axis, pairs)]
    ppermute x0 -> x3, starting transfers between devices: none -> 2.03 us  [head_over_rep(): lax.ppermute(send.astype(jnp.bfloat16), 'rep', pairs).astype(jnp.float32)]
    ppermute x11 -> x9, starting transfers between devices: 10 us -> 8.7 us  [swapped(): return lax.ppermute(value, axis, pairs)]
    unnamed x38 -> x39, local copies, waits for them, and re-layouts: 3.91 us -> 3.66 us
  transfers between devices with their start and end apart: 15 -> 16, of which waited for: 12 -> 11; matrix products, arithmetic and copies ran while one was open for 26% -> 24% of each run, Pallas kernels for 0% -> 0%
where the time goes in v3:
time: 178 us; the launch traced here: 177 us
  waiting for transfers between devices  105 us (59%)
  matrix products  36.5 us (21%)
  starting transfers between devices  18.4 us (10%)
  other arithmetic  10 us (6%)
  local copies, waits for them, and re-layouts  4.67 us (3%)
  between operations  2.63 us (1%)
    ppermute x4, waiting for transfers between devices, shifted(): return lax.ppermute(value, axis, pairs)  41.9 us
    ppermute x9, waiting for transfers between devices, swapped(): return lax.ppermute(value, axis, pairs)  38.5 us
    ppermute x3, waiting for transfers between devices, head_over_rep(): lax.ppermute(send.astype(jnp.bfloat16), 'rep', pairs).astype(jnp.float32)  24.3 us
    dot_general x9, matrix products, coefficients(): jnp.einsum('id,jd->ij', rows, columns, preferred_element_type=jnp.float32)  14 us
    ppermute x9, starting transfers between devices, swapped(): return lax.ppermute(value, axis, pairs)  8.7 us
    ppermute x4, starting transfers between devices, shifted(): return lax.ppermute(value, axis, pairs)  7.65 us
    dot_general x4, matrix products, image_part(): return jnp.dot(coef, texts, preferred_element_type=jnp.float32)  7.46 us
    dot_general x4, matrix products, text_part(): return jnp.dot(coef, images, preferred_element_type=jnp.float32)  3.82 us
  transfers between devices with their start and end apart: 16, of which 11 were waited for; matrix products, arithmetic and copies ran while one was open for 24% of the time, Pallas kernels for 0%

profile of v3, /device:TPU:0, one launch (start us, length us, event | category | flops | bytes accessed | tf_op | source)
XLA Modules:
  0.0 176.9 jit_solution(1678532791410733892)
XLA Ops:
  0.7 1.7 fusion.7
  3.3 3.1 %collective-permute-start = (bf16[520,1152]{1,0:T(8,128)(2,1)S(1)}, bf16[520,1152]{1,0:T(8,128)(2,1)}, u32[]{:S(2)}, u32[]{:S(2)}) collective-permute-start(bf16[520,1152]{1,0:T(8,128)(2,1)S(1)} %pad_maximum_fusion), channel_id=1, source_target_pairs={{0,8},{4,12},{8,16},{12,20},{16,24},{20,28},{24,0},{28,4},{1,9},{5... | collective-permute-start | bytes 3594248 | tf_op jit(solution)/shard_map/ppermute | solution.py:12
  6.4 1.9 %multiply_reduce_fusion.1 = (f32[512]{0:T(512)S(1)}, f32[512,1152]{1,0:T(8,128)S(1)}) fusion(bf16[512,1152]{1,0:T(8,128)(2,1)S(1)} %copy-done.14, bf16[1152,1152]{1,0:T(8,128)(2,1)S(1)} %copy-done), kind=kOutput, calls=%fused_computation.15 | convolution fusion | flops 1360133632 | bytes 6195200 | tf_op jit(solution)/shard_map/dot_general | solution.py:123
  12.3 2.3 %fusion.127 = f32[512,1152]{1,0:T(8,128)} fusion(bf16[512,512]{1,0:T(8,128)(2,1)S(1)} %fusion.73, bf16[512,1152]{1,0:T(8,128)(2,1)S(1)} %multiply_convert_fusion.1), kind=kOutput, calls=%fused_computation.209 | convolution fusion | flops 603979776 | bytes 4063232 | tf_op jit(solution)/shard_map/ij,id->jd/dot_general | solution.py:129
  14.6 2.3 %fusion.126 = f32[512,1152]{1,0:T(8,128)} fusion(bf16[512,512]{1,0:T(8,128)(2,1)S(1)} %fusion.73, bf16[512,1152]{1,0:T(8,128)(2,1)S(1)} %fusion.2), kind=kOutput, calls=%fused_computation.208 | convolution fusion | flops 603979776 | bytes 4063232 | tf_op jit(solution)/shard_map/dot_general | solution.py:128
  16.9 17.9 %collective-permute-done = bf16[520,1152]{1,0:T(8,128)(2,1)} collective-permute-done((bf16[520,1152]{1,0:T(8,128)(2,1)S(1)}, bf16[520,1152]{1,0:T(8,128)(2,1)}, u32[]{:S(2)}, u32[]{:S(2)}) %collective-permute-start) | collective-permute-done | bytes 1198112 | tf_op jit(solution)/shard_map/ppermute | solution.py:12
  34.8 1.5 collective-permute-start.2
  37.1 2.7 %fusion.74 = bf16[512,512]{1,0:T(8,128)(2,1)S(1)} fusion(bf16[512,1152]{1,0:T(8,128)(2,1)} %copy-done.7, bf16[520,1152]{1,0:T(8,128)(2,1)} %collective-permute-done, f32[512]{0:T(512)S(1)} %bitcast.60, f32[]{:T(128)} %bitcast.52, f32[]{:T(128)} %bitcast, f32[512]{0:T(512)S(1)} %get-tuple-element.42), kind=kOutput, calls=%fused_computation.96 | convolution fusion | flops 606601216 | bytes 2888704 | tf_op jit(solution)/shard_map/id,jd->ij/dot_general | solution.py:102
  39.8 2.3 %fusion.104 = f32[512,1152]{1,0:T(8,128)S(1)} fusion(bf16[512,512]{1,0:T(8,128)(2,1)S(1)} %fusion.74, bf16[520,1152]{1,0:T(8,128)(2,1)} %collective-permute-done), kind=kOutput, calls=%fused_computation.128 | convolution fusion | flops 603979776 | bytes 4063232 | tf_op jit(solution)/shard_map/dot_general | solution.py:112
  42.4 22.1 %collective-permute-done.1 = bf16[520,1152]{1,0:T(8,128)(2,1)} collective-permute-done((bf16[520,1152]{1,0:T(8,128)(2,1)}, bf16[520,1152]{1,0:T(8,128)(2,1)}, u32[]{:S(2)}, u32[]{:S(2)}) %collective-permute-start.1) | collective-permute-done | bytes 1198112 | tf_op jit(solution)/shard_map/ppermute | solution.py:12
  65.5 2.8 %collective-permute-start.4 = (bf16[520,1152]{1,0:T(8,128)(2,1)S(1)}, bf16[520,1152]{1,0:T(8,128)(2,1)S(1)}, u32[]{:S(2)}, u32[]{:S(2)}) collective-permute-start(bf16[520,1152]{1,0:T(8,128)(2,1)S(1)} %broadcast_select_fusion.1), channel_id=1, source_target_pairs={{0,4},{4,0},{8,12},{12,8},{16,20},{20,16},{24,28},{28,24},{1,5},{5... | collective-permute-start | bytes 3594248 | tf_op jit(solution)/shard_map/ppermute | solution.py:18
  68.2 1.7 collective-permute-start.3
  70.0 2.4 %fusion.76 = bf16[512,512]{1,0:T(8,128)(2,1)S(1)} fusion(bf16[512,1152]{1,0:T(8,128)(2,1)S(1)} %copy-done.8, bf16[520,1152]{1,0:T(8,128)(2,1)} %collective-permute-done.1, f32[512]{0:T(512)S(1)} %bitcast.57, f32[]{:T(128)} %bitcast.50, f32[]{:T(128)} %bitcast, f32[512]{0:T(512)S(1)} %get-tuple-element.42), kind=kOutput, calls=%fused_computation.98 | convolution fusion | flops 606601216 | bytes 2888704 | tf_op jit(solution)/shard_map/id,jd->ij/dot_general | solution.py:102
  72.4 2.4 %fusion.75 = bf16[512,512]{1,0:T(8,128)(2,1)S(1)} fusion(bf16[512,1152]{1,0:T(8,128)(2,1)S(1)} %copy-done.8, bf16[520,1152]{1,0:T(8,128)(2,1)} %collective-permute-done.2, f32[512]{0:T(512)S(1)} %bitcast.61, f32[]{:T(128)} %bitcast.51, f32[]{:T(128)} %bitcast, f32[512]{0:T(512)S(1)} %get-tuple-element.42), kind=kOutput, calls=%fused_computation.97 | convolution fusion | flops 606601216 | bytes 2888704 | tf_op jit(solution)/shard_map/id,jd->ij/dot_general | solution.py:102
  74.7 2.1 %fusion.101 = f32[512,1152]{1,0:T(8,128)S(1)} fusion(bf16[512,512]{1,0:T(8,128)(2,1)S(1)} %fusion.75, bf16[520,1152]{1,0:T(8,128)(2,1)} %collective-permute-done.2), kind=kOutput, calls=%fused_computation.125 | convolution fusion | flops 603979776 | bytes 4063232 | tf_op jit(solution)/shard_map/dot_general | solution.py:112
  76.8 2.2 %add_add_fusion = f32[512,1152]{1,0:T(8,128)S(1)} fusion(f32[512,1152]{1,0:T(8,128)S(1)} %add.241, f32[512,1152]{1,0:T(8,128)S(1)} %fusion.101, bf16[512,512]{1,0:T(8,128)(2,1)S(1)} %fusion.76, bf16[520,1152]{1,0:T(8,128)(2,1)} %collective-permute-done.1), kind=kOutput, calls=%fused_computation.14 | convolution fusion | flops 605159424 | bytes 8781824 | tf_op jit(solution)/shard_map/dot_general | solution.py:112
  79.1 13.8 %collective-permute-done.4 = bf16[520,1152]{1,0:T(8,128)(2,1)S(1)} collective-permute-done((bf16[520,1152]{1,0:T(8,128)(2,1)S(1)}, bf16[520,1152]{1,0:T(8,128)(2,1)S(1)}, u32[]{:S(2)}, u32[]{:S(2)}) %collective-permute-start.4) | collective-permute-done | bytes 1198112 | tf_op jit(solution)/shard_map/ppermute | solution.py:18
  92.9 1.9 %collective-permute-done.3 = bf16[520,1152]{1,0:T(8,128)(2,1)S(1)} collective-permute-done((bf16[520,1152]{1,0:T(8,128)(2,1)S(1)}, bf16[520,1152]{1,0:T(8,128)(2,1)S(1)}, u32[]{:S(2)}, u32[]{:S(2)}) %collective-permute-start.3) | collective-permute-done | bytes 1198112 | tf_op jit(solution)/shard_map/ppermute | solution.py:12
  94.8 2.8 %collective-permute-start.5 = (bf16[520,1152]{1,0:T(8,128)(2,1)S(1)}, bf16[520,1152]{1,0:T(8,128)(2,1)S(1)}, u32[]{:S(2)}, u32[]{:S(2)}) collective-permute-start(bf16[520,1152]{1,0:T(8,128)(2,1)S(1)} %collective-permute-done.3), channel_id=1, source_target_pairs={{0,24},{4,28},{8,0},{12,4},{16,8},{20,12},{24,16},{28,20},{1,25},{... | collective-permute-start | bytes 3594248 | tf_op jit(solution)/shard_map/ppermute | solution.py:12
  100.2 1.4 copy-done.2
  103.2 1.8 fusion.128
  105.7 1.5 collective-permute-start.8
  109.9 2.9 %convolution_convert_fusion = bf16[512,1152]{1,0:T(8,128)(2,1)} fusion(bf16[512,1152]{1,0:T(8,128)(2,1)S(1)} %multiply_convert_fusion, bf16[1152,1152]{1,0:T(8,128)(2,1)S(1)} %copy-done), kind=kOutput, calls=%fused_computation.1 | convolution fusion | flops 1359544320 | bytes 5013504 | tf_op jit(solution)/shard_map/id,ed->ie/dot_general | solution.py:151
  112.7 10.1 %collective-permute-done.7 = bf16[8,36,1152]{2,0,1:T(8,128)(2,1)S(1)} collective-permute-done((bf16[8,36,1152]{2,0,1:T(8,128)(2,1)S(1)}, bf16[8,36,1152]{2,0,1:T(8,128)(2,1)S(1)}, u32[]{:S(2)}, u32[]{:S(2)}) %collective-permute-start.7) | collective-permute-done | bytes 663584 | tf_op jit(solution)/shard_map/ppermute | solution.py:60
  122.8 14.3 %collective-permute-done.8 = bf16[8,36,1152]{2,0,1:T(8,128)(2,1)S(1)} collective-permute-done((bf16[8,36,1152]{2,0,1:T(8,128)(2,1)S(1)}, bf16[8,36,1152]{2,0,1:T(8,128)(2,1)S(1)}, u32[]{:S(2)}, u32[]{:S(2)}) %collective-permute-start.8) | collective-permute-done | bytes 663584 | tf_op jit(solution)/shard_map/ppermute | solution.py:60
  138.0 1.7 collective-permute-start.10
  141.9 6.6 %collective-permute-done.11 = bf16[2,1,2,36,1152]{4,3,2,1,0:T(8,128)(2,1)S(1)} collective-permute-done((bf16[2,1,2,36,1152]{4,3,2,1,0:T(8,128)(2,1)S(1)}, bf16[2,1,2,36,1152]{4,3,2,1,0:T(8,128)(2,1)S(1)}, u32[]{:S(2)}, u32[]{:S(2)}) %collective-permute-start.11) | collective-permute-done | bytes 331808 | tf_op jit(solution)/shard_map/ppermute | solution.py:18
  149.6 9.8 %collective-permute-done.12 = bf16[1,1,2,36,1152]{4,3,2,1,0:T(8,128)(2,1)S(1)} collective-permute-done((bf16[1,1,2,36,1152]{4,3,2,1,0:T(8,128)(2,1)S(1)}, bf16[1,1,2,36,1152]{4,3,2,1,0:T(8,128)(2,1)S(1)}, u32[]{:S(2)}, u32[]{:S(2)}) %collective-permute-start.12) | collective-permute-done | bytes 165920 | tf_op jit(solution)/shard_map/ppermute | solution.py:18
  159.4 1.7 collective-permute-start.13
  162.2 6.2 %collective-permute-done.13 = bf16[1,1,1,36,1152]{4,3,2,1,0:T(8,128)(2,1)S(1)} collective-permute-done((bf16[1,1,1,36,1152]{4,3,2,1,0:T(8,128)(2,1)S(1)}, bf16[1,1,1,36,1152]{4,3,2,1,0:T(8,128)(2,1)S(1)}, u32[]{:S(2)}, u32[]{:S(2)}) %collective-permute-start.13) | collective-permute-done | bytes 82976 | tf_op jit(solution)/shard_map/ppermute | solution.py:18
  172.2 2.0 %collective-permute-done.14 = f32[36,1152]{1,0:T(8,128)S(1)} collective-permute-done((f32[36,1152]{1,0:T(8,128)S(1)}, f32[36,1152]{1,0:T(8,128)S(1)}, u32[]{:S(2)}, u32[]{:S(2)}) %collective-permute-start.14) | collective-permute-done | bytes 165920 | tf_op jit(solution)/shard_map/ppermute | solution.py:18
  174.4 1.5 fusion.6
  (113 shorter events, 22.8 us)
Async XLA Ops:
  0.6 5.7 %copy-start = (bf16[1152,1152]{1,0:T(8,128)(2,1)S(1)}, bf16[1152,1152]{1,0:T(8,128)(2,1)}, u32[]{:S(2)}) copy-start(bf16[1152,1152]{1,0:T(8,128)(2,1)} %param.9) | copy-start | bytes 7962628
  0.6 1.8 %copy-start.3 = (bf16[512,1152]{1,0:T(8,128)(2,1)S(1)}, bf16[512,1152]{1,0:T(8,128)(2,1)}, u32[]{:S(2)}) copy-start(bf16[512,1152]{1,0:T(8,128)(2,1)} %param.8) | copy-start | bytes 3538948
  3.1 11.5 %copy-start.9 = (bf16[512,1152]{1,0:T(8,128)(2,1)}, bf16[512,1152]{1,0:T(8,128)(2,1)S(1)}, u32[]{:S(2)}) copy-start(bf16[512,1152]{1,0:T(8,128)(2,1)S(1)} %fusion.2) | copy-start | bytes 3538948
  3.1 3.2 %copy-start.14 = (bf16[512,1152]{1,0:T(8,128)(2,1)S(1)}, bf16[512,1152]{1,0:T(8,128)(2,1)}, u32[]{:S(2)}) copy-start(bf16[512,1152]{1,0:T(8,128)(2,1)} %param.7) | copy-start | bytes 3538948
  3.3 5.1 %copy-start.12 = (bf16[520,1152]{1,0:T(8,128)(2,1)}, bf16[520,1152]{1,0:T(8,128)(2,1)S(1)}, u32[]{:S(2)}) copy-start(bf16[520,1152]{1,0:T(8,128)(2,1)S(1)} %pad_maximum_fusion) | copy-start | bytes 3594244
  3.3 6.5 %copy-start.17 = (s32[512]{0:T(512)S(1)}, s32[512]{0:T(512)}, u32[]{:S(2)}) copy-start(s32[512]{0:T(512)} %param.10) | copy-start | bytes 6148
  3.3 31.6 %collective-permute-start = (bf16[520,1152]{1,0:T(8,128)(2,1)S(1)}, bf16[520,1152]{1,0:T(8,128)(2,1)}, u32[]{:S(2)}, u32[]{:S(2)}) collective-permute-start(bf16[520,1152]{1,0:T(8,128)(2,1)S(1)} %pad_maximum_fusion), channel_id=1, source_target_pairs={{0,8},{4,12},{8,16},{12,20},{16,24},{20,28},{24,0},{28,4},{1,9},{5... | collective-permute-start | bytes 3594248 | tf_op jit(solution)/shard_map/ppermute | solution.py:12
  8.3 1.7 copy-start.1
  10.0 2.3 %copy-start.7 = (bf16[512,1152]{1,0:T(8,128)(2,1)}, bf16[512,1152]{1,0:T(8,128)(2,1)S(1)}, u32[]{:S(2)}) copy-start(bf16[512,1152]{1,0:T(8,128)(2,1)S(1)} %multiply_convert_fusion.1) | copy-start | bytes 3538948
  34.8 29.7 %collective-permute-start.1 = (bf16[520,1152]{1,0:T(8,128)(2,1)}, bf16[520,1152]{1,0:T(8,128)(2,1)}, u32[]{:S(2)}, u32[]{:S(2)}) collective-permute-start(bf16[520,1152]{1,0:T(8,128)(2,1)} %collective-permute-done), channel_id=1, source_target_pairs={{0,8},{4,12},{8,16},{12,20},{16,24},{20,28},{24,0},{28,4},{1,9},{5... | collective-permute-start | bytes 3594248 | tf_op jit(solution)/shard_map/ppermute | solution.py:12
  34.8 29.7 %collective-permute-start.2 = (bf16[520,1152]{1,0:T(8,128)(2,1)}, bf16[520,1152]{1,0:T(8,128)(2,1)}, u32[]{:S(2)}, u32[]{:S(2)}) collective-permute-start(bf16[520,1152]{1,0:T(8,128)(2,1)} %collective-permute-done), channel_id=1, source_target_pairs={{0,4},{4,0},{8,12},{12,8},{16,20},{20,16},{24,28},{28,24},{1,5},{5... | collective-permute-start | bytes 3594248 | tf_op jit(solution)/shard_map/ppermute | solution.py:18
  39.8 2.3 %copy-start.6 = (f32[512,1152]{1,0:T(8,128)S(1)}, f32[512,1152]{1,0:T(8,128)}, u32[]{:S(2)}) copy-start(f32[512,1152]{1,0:T(8,128)} %fusion.126) | copy-start | bytes 7077892
  42.1 23.1 %copy-start.13 = (bf16[520,1152]{1,0:T(8,128)(2,1)S(1)}, bf16[520,1152]{1,0:T(8,128)(2,1)}, u32[]{:S(2)}) copy-start(bf16[520,1152]{1,0:T(8,128)(2,1)} %copy-done.12) | copy-start | bytes 3594244
  65.3 3.0 %copy-start.11 = (bf16[520,1152]{1,0:T(8,128)(2,1)S(1)}, bf16[520,1152]{1,0:T(8,128)(2,1)}, u32[]{:S(2)}) copy-start(bf16[520,1152]{1,0:T(8,128)(2,1)} %pad_maximum_fusion.1) | copy-start | bytes 3594244
  65.3 4.7 %copy-start.8 = (bf16[512,1152]{1,0:T(8,128)(2,1)S(1)}, bf16[512,1152]{1,0:T(8,128)(2,1)}, u32[]{:S(2)}) copy-start(bf16[512,1152]{1,0:T(8,128)(2,1)} %copy-done.7) | copy-start | bytes 3538948
  65.5 27.4 %collective-permute-start.4 = (bf16[520,1152]{1,0:T(8,128)(2,1)S(1)}, bf16[520,1152]{1,0:T(8,128)(2,1)S(1)}, u32[]{:S(2)}, u32[]{:S(2)}) collective-permute-start(bf16[520,1152]{1,0:T(8,128)(2,1)S(1)} %broadcast_select_fusion.1), channel_id=1, source_target_pairs={{0,4},{4,0},{8,12},{12,8},{16,20},{20,16},{24,28},{28,24},{1,5},{5... | collective-permute-start | bytes 3594248 | tf_op jit(solution)/shard_map/ppermute | solution.py:18
  68.2 26.5 %collective-permute-start.3 = (bf16[520,1152]{1,0:T(8,128)(2,1)S(1)}, bf16[520,1152]{1,0:T(8,128)(2,1)S(1)}, u32[]{:S(2)}, u32[]{:S(2)}) collective-permute-start(bf16[520,1152]{1,0:T(8,128)(2,1)S(1)} %copy-done.11), channel_id=1, source_target_pairs={{0,24},{4,28},{8,0},{12,4},{16,8},{20,12},{24,16},{28,20},{1,25},{... | collective-permute-start | bytes 3594248 | tf_op jit(solution)/shard_map/ppermute | solution.py:12
  94.8 42.6 %collective-permute-start.5 = (bf16[520,1152]{1,0:T(8,128)(2,1)S(1)}, bf16[520,1152]{1,0:T(8,128)(2,1)S(1)}, u32[]{:S(2)}, u32[]{:S(2)}) collective-permute-start(bf16[520,1152]{1,0:T(8,128)(2,1)S(1)} %collective-permute-done.3), channel_id=1, source_target_pairs={{0,24},{4,28},{8,0},{12,4},{16,8},{20,12},{24,16},{28,20},{1,25},{... | collective-permute-start | bytes 3594248 | tf_op jit(solution)/shard_map/ppermute | solution.py:12
  97.6 39.8 %collective-permute-start.6 = (bf16[520,1152]{1,0:T(8,128)(2,1)S(1)}, bf16[520,1152]{1,0:T(8,128)(2,1)S(1)}, u32[]{:S(2)}, u32[]{:S(2)}) collective-permute-start(bf16[520,1152]{1,0:T(8,128)(2,1)S(1)} %collective-permute-done.3), channel_id=1, source_target_pairs={{0,4},{4,0},{8,12},{12,8},{16,20},{20,16},{24,28},{28,24},{1,5},{5... | collective-permute-start | bytes 3594248 | tf_op jit(solution)/shard_map/ppermute | solution.py:18
  99.9 1.7 copy-start.2
  101.9 1.3 copy-start.15
  105.6 17.2 %collective-permute-start.7 = (bf16[8,36,1152]{2,0,1:T(8,128)(2,1)S(1)}, bf16[8,36,1152]{2,0,1:T(8,128)(2,1)S(1)}, u32[]{:S(2)}, u32[]{:S(2)}) collective-permute-start(bf16[8,36,1152]{2,0,1:T(8,128)(2,1)S(1)} %copy.31), channel_id=1, source_target_pairs={{0,3},{1,2},{2,1},{3,0},{4,7},{5,6},{6,5},{7,4},{8,11},{9,10},{10,... | collective-permute-start | bytes 1990664 | tf_op jit(solution)/shard_map/ppermute | solution.py:60
  105.6 2.1 %copy-start.10 = (bf16[512,1152]{1,0:T(8,128)(2,1)S(1)}, bf16[512,1152]{1,0:T(8,128)(2,1)}, u32[]{:S(2)}) copy-start(bf16[512,1152]{1,0:T(8,128)(2,1)} %copy-done.9) | copy-start | bytes 3538948
  105.7 31.3 %collective-permute-start.8 = (bf16[8,36,1152]{2,0,1:T(8,128)(2,1)S(1)}, bf16[8,36,1152]{2,0,1:T(8,128)(2,1)S(1)}, u32[]{:S(2)}, u32[]{:S(2)}) collective-permute-start(bf16[8,36,1152]{2,0,1:T(8,128)(2,1)S(1)} %copy.30), channel_id=1, source_target_pairs={{0,2},{1,3},{2,0},{3,1},{4,6},{5,7},{6,4},{7,5},{8,10},{9,11},{10,... | collective-permute-start | bytes 1990664 | tf_op jit(solution)/shard_map/ppermute | solution.py:60
  107.4 29.7 %collective-permute-start.9 = (bf16[8,36,1152]{2,0,1:T(8,128)(2,1)S(1)}, bf16[8,36,1152]{2,0,1:T(8,128)(2,1)S(1)}, u32[]{:S(2)}, u32[]{:S(2)}) collective-permute-start(bf16[8,36,1152]{2,0,1:T(8,128)(2,1)S(1)} %copy.29), channel_id=1, source_target_pairs={{0,1},{1,0},{2,3},{3,2},{4,5},{5,4},{6,7},{7,6},{8,9},{9,8},{10,11... | collective-permute-start | bytes 1990664 | tf_op jit(solution)/shard_map/ppermute | solution.py:60
  137.9 10.6 %collective-permute-start.11 = (bf16[2,1,2,36,1152]{4,3,2,1,0:T(8,128)(2,1)S(1)}, bf16[2,1,2,36,1152]{4,3,2,1,0:T(8,128)(2,1)S(1)}, u32[]{:S(2)}, u32[]{:S(2)}) collective-permute-start(bf16[2,1,2,36,1152]{4,3,2,1,0:T(8,128)(2,1)S(1)} %dynamic-slice_convert_fusion), channel_id=1, source_target_pairs={{0,8},{4,12},{8,0},{12,4},{16,24},{20,28},{24,16},{28,20},{1,9},{5... | collective-permute-start | bytes 995336 | tf_op jit(solution)/shard_map/ppermute | solution.py:18
  138.0 30.4 %collective-permute-start.10 = (bf16[520,1152]{1,0:T(8,128)(2,1)S(1)}, bf16[520,1152]{1,0:T(8,128)(2,1)S(1)}, u32[]{:S(2)}, u32[]{:S(2)}) collective-permute-start(bf16[520,1152]{1,0:T(8,128)(2,1)S(1)} %broadcast_select_fusion), channel_id=1, source_target_pairs={{0,4},{4,0},{8,12},{12,8},{16,20},{20,16},{24,28},{28,24},{1,5},{5... | collective-permute-start | bytes 3594248 | tf_op jit(solution)/shard_map/ppermute | solution.py:18
  148.6 10.7 %collective-permute-start.12 = (bf16[1,1,2,36,1152]{4,3,2,1,0:T(8,128)(2,1)S(1)}, bf16[1,1,2,36,1152]{4,3,2,1,0:T(8,128)(2,1)S(1)}, u32[]{:S(2)}, u32[]{:S(2)}) collective-permute-start(bf16[1,1,2,36,1152]{4,3,2,1,0:T(8,128)(2,1)S(1)} %dynamic-slice_convert_fusion.1), channel_id=1, source_target_pairs={{0,16},{4,20},{8,24},{12,28},{16,0},{20,4},{24,8},{28,12},{1,17},{... | collective-permute-start | bytes 497672 | tf_op jit(solution)/shard_map/ppermute | solution.py:18
  159.4 9.0 %collective-permute-start.13 = (bf16[1,1,1,36,1152]{4,3,2,1,0:T(8,128)(2,1)S(1)}, bf16[1,1,1,36,1152]{4,3,2,1,0:T(8,128)(2,1)S(1)}, u32[]{:S(2)}, u32[]{:S(2)}) collective-permute-start(bf16[1,1,1,36,1152]{4,3,2,1,0:T(8,128)(2,1)S(1)} %dynamic-slice_convert_fusion.2), channel_id=1, source_target_pairs={{0,4},{4,0},{8,12},{12,8},{16,20},{20,16},{24,28},{28,24},{1,5},{5... | collective-permute-start | bytes 248840 | tf_op jit(solution)/shard_map/ppermute | solution.py:18
  168.4 5.8 %collective-permute-start.14 = (f32[36,1152]{1,0:T(8,128)S(1)}, f32[36,1152]{1,0:T(8,128)S(1)}, u32[]{:S(2)}, u32[]{:S(2)}) collective-permute-start(f32[36,1152]{1,0:T(8,128)S(1)} %multiply_bitcast_fusion), channel_id=1, source_target_pairs={{0,2},{1,3},{2,0},{3,1},{4,6},{5,7},{6,4},{7,5},{8,10},{9,11},{10,... | collective-permute-start | bytes 497672 | tf_op jit(solution)/shard_map/ppermute | solution.py:18
  168.8 1.7 copy-start.5
  174.3 1.7 collective-permute-start.15
  (2 other events, 2.0 us)
